TPU v7x, 32 devices: a whole 2x2x4 slice. The times are simulated.
32 devices in a mesh: band: 8 (over y, x, core), plane: 4 (over z).
Axes of the slice: x: 2, y: 2, z: 4, core: 2. Of those that a mesh axis runs over, the one named last changes fastest.
Arguments:
- orbitals: bfloat16 [64, 128, 128, 128], P('band', 'plane'), may hold values from -6 to 6
- potential_slots: bfloat16 [8, 2, 128, 128, 128], P('band', None, 'plane'), may hold values from -6 to 6
- pattern_owner: int32 [4], replicated, may hold values from 0 to 7, as said below
- retained: int32 [3, 64], replicated, may hold values from 0 to 127, as said below
- band_energy: float32 [64], P('band'), may hold values from 0.5 to 8
Outputs:
- rhs: float32 [64, 4, 64, 64, 128], P('band', None, None, 'plane')
Inputs may be any that keep to these rules, and one draw needn't show every extreme that they name: pattern_owner holds 4 distinct slot indices. Each row of retained holds 64 distinct frequency indices.
All inputs are finite; a program needn't handle non-finite values.
Results may differ from a plain program's by a relative error of at most 0.0003.
Values may be sent and summed in bfloat16 or wider, within the bound.
No kernel may reach another device: no remote copies, remote signals or barrier semaphores. Data moves between devices by JAX's collectives and lax.ppermute only.
A program may use at most 192 MiB of HBM per device.

v0:
```python
import math

import jax
import jax.numpy as jnp
from jax import lax
from jax.sharding import PartitionSpec as P

kinetic_coef = 0.5 * (2.0 * math.pi / 64.0) ** 2


def broadcast(block, axis, holder):
    block = jnp.where(lax.axis_index(axis) == holder, block, jnp.zeros_like(block))
    return lax.psum(block, axis)


def make_table(frequency, length):
    position = jnp.arange(length, dtype=jnp.int32)
    phase_index = position[:, None] * frequency[None, :] % length
    angles = phase_index.astype(jnp.float32) * (2.0 * math.pi / length)
    norm_factor = 1.0 / math.sqrt(length)
    return jnp.concatenate([jnp.cos(angles), -jnp.sin(angles)], axis=1) * norm_factor


def signed_square(frequency, length):
    signed = jnp.where(frequency < length // 2, frequency, frequency - length).astype(jnp.float32)
    return signed * signed


def fetch_potential(potential_slots, slot_index):
    return broadcast(potential_slots, "band", slot_index)


def per_device(orbitals, potential_slots, pattern_owner, retained, band_energy):
    length = orbitals.shape[2]
    kept_count = retained.shape[1]
    highest = lax.Precision.HIGHEST
    table_x = make_table(retained[0], length)
    table_y = make_table(retained[1], length)
    table_z = make_table(retained[2], length)
    plane_rank = lax.axis_index("plane")
    plane_count = lax.axis_size("plane")
    local_keep = kept_count // plane_count
    ky_local = lax.dynamic_slice_in_dim(retained[1], plane_rank * local_keep, local_keep)
    kinetic = kinetic_coef * (
        signed_square(retained[0], length)[:, None, None]
        + signed_square(ky_local, length)[None, :, None]
        + signed_square(retained[2], length)[None, None, :]
    )
    precond = 1.0 / (1.0 + kinetic[None] / band_energy[:, None, None, None])
    results = []
    for pattern in range(pattern_owner.shape[0]):
        potential = fetch_potential(potential_slots, pattern_owner[pattern])
        planar_potential = potential[0]
        product = orbitals[None].astype(jnp.float32) * planar_potential[:, None].astype(jnp.float32)
        along_z = jnp.dot(product.reshape(-1, length), table_z, precision=highest).reshape(
            product.shape[:-1] + (2 * kept_count,)
        )
        mixed_z = jnp.concatenate(
            [
                along_z[0, ..., :kept_count] - along_z[1, ..., kept_count:],
                along_z[0, ..., kept_count:] + along_z[1, ..., :kept_count],
            ],
            axis=-1,
        )
        along_y = jnp.einsum("yj,bxyc->bxjc", table_y, mixed_z, precision=highest)
        planes = jnp.concatenate(
            [
                along_y[:, :, :kept_count, :kept_count] - along_y[:, :, kept_count:, kept_count:],
                along_y[:, :, kept_count:, :kept_count] + along_y[:, :, :kept_count, kept_count:],
            ],
            axis=-1,
        )[:, None]
        along_x = jnp.einsum(
            "xi,bpxjc->bpijc",
            table_x,
            lax.all_to_all(planes, "plane", split_axis=3, concat_axis=2, tiled=True),
            precision=highest,
        )
        real_part = (
            along_x[:, :, :kept_count, :, :kept_count] - along_x[:, :, kept_count:, :, kept_count:]
        )
        imag_part = (
            along_x[:, :, kept_count:, :, :kept_count] + along_x[:, :, :kept_count, :, kept_count:]
        )
        results.append(
            jnp.concatenate([real_part * precond[:, None], imag_part * precond[:, None]], axis=-1)
        )
    return jnp.concatenate(results, axis=1)


def solution(mesh):
    in_specs = (
        P("band", "plane", None, None),
        P("band", None, "plane", None, None),
        P(),
        P(),
        P("band"),
    )
    out_specs = P("band", None, None, "plane", None)
    return jax.shard_map(
        per_device, mesh=mesh, in_specs=in_specs, out_specs=out_specs, check_vma=False
    )
```

profile of v0, /device:TPU:0, one launch (start us, length us, event | category | flops | bytes accessed | tf_op | source)
XLA Modules:
  0.0 1104.7 jit_solution(11134766358744772368)
XLA Ops:
  6.5 1.4 fusion.128
  10.4 5.0 select_bitcast_fusion.3
  15.5 11.8 %convert_element_type.81 = f32[8,32,128,128]{3,2,1,0:T(8,128)} convert(bf16[8,32,128,128]{3,2,1,0:T(8,128)(2,1)} %param.5) | non-fusion elementwise | flops 4194304 | bytes 25165824 | tf_op jit(solution)/shard_map/convert_element_type | solution.py:54
  28.3 117.6 %all-reduce.3.cloned.1.call-done = (bf16[2,32,128,128]{3,2,1,0:T(8,128)(2,1)}, bf16[2,32,128,128]{3,2,1,0:T(8,128)(2,1)}, bf16[2,32,128,128]{3,2,1,0:T(8,128)(2,1)}, bf16[2,32,128,128]{3,2,1,0:T(8,128)(2,1)}) async-done(((bf16[2,32,128,128]{3,2,1,0:T(8,128)(2,1)}, bf16[2,32,128,128]{3,2,1,0:T(8,128)(2,1)}, bf16[2,32,128,128]{3,2,1,0:T(8,128)(2,1)}, bf16[2,32,128,128]{3,2,1,0:T(8,128)(2,1)}), ...) | async-done | bytes 8388624 | tf_op jit(solution)/shard_map/psum | solution.py:13
  145.8 2.1 convert_element_type.95
  147.9 38.9 %fusion = f32[2,8,32,128,128]{3,4,2,1,0:T(8,128)} fusion(f32[2,32,128,128]{3,2,1,0:T(8,128)S(1)} %convert_element_type.95, f32[8,32,128,128]{3,2,1,0:T(8,128)} %convert_element_type.81, f32[128,64]{0,1:T(8,128)S(1)} %get-tuple-element.54, f32[128,64]{0,1:T(8,128)S(1)} %get-tuple-element.53), kind=kOutput, calls=%fused_computation | convolution fusion | flops 12893323264 | bytes 54591488 | tf_op jit(solution)/shard_map/dot_general | solution.py:55
  186.9 18.9 %fusion.45 = (f32[8,32,128,64]{2,3,1,0:T(8,128)}, f32[8,32,128,64]{2,3,1,0:T(8,128)}) fusion(f32[2,8,32,128,128]{3,4,2,1,0:T(8,128)} %fusion), kind=kLoop, calls=%fused_computation.42 | loop fusion | flops 4194304 | bytes 50331648 | tf_op jit(solution)/shard_map/sub | solution.py:60
  205.7 22.3 %fusion.32 = f32[8,32,128,128]{3,2,1,0:T(8,128)} fusion(f32[8,32,128,64]{2,3,1,0:T(8,128)} %get-tuple-element.16, f32[8,32,128,64]{2,3,1,0:T(8,128)} %get-tuple-element.15, f32[128,64]{0,1:T(8,128)S(1)} %get-tuple-element.52, f32[128,64]{0,1:T(8,128)S(1)} %get-tuple-element.51), kind=kOutput, calls=%fused_computation.33 | convolution fusion | flops 6446678016 | bytes 33619968 | tf_op jit(solution)/shard_map/yj,bxyc->bxjc/dot_general | solution.py:65
  228.0 19.2 %slice_subtract_fusion = (f32[8,32,64,64]{3,2,1,0:T(8,128)}, f32[8,32,64,64]{3,2,1,0:T(8,128)}) fusion(f32[8,32,128,128]{3,2,1,0:T(8,128)} %fusion.32), kind=kLoop, calls=%fused_computation.38 | loop fusion | flops 2097152 | bytes 25165824 | tf_op jit(solution)/shard_map/sub | solution.py:68
  247.2 11.9 %maximum_bitcast_fusion.3 = f32[8,1,32,64,128]{4,3,2,0,1:T(8,128)} fusion(f32[8,32,64,64]{3,2,1,0:T(8,128)} %get-tuple-element.24, f32[8,32,64,64]{3,2,1,0:T(8,128)} %get-tuple-element.23), kind=kLoop, calls=%fused_computation.64 | loop fusion | flops 2097152 | bytes 16777216 | tf_op jit(solution)/shard_map/broadcast_in_dim | solution.py:66
  259.2 11.5 %copy.25 = f32[8,1,32,64,128]{4,2,0,1,3:T(8,128)} copy(f32[8,1,32,64,128]{4,3,2,0,1:T(8,128)} %maximum_bitcast_fusion.3) | data formatting | bytes 16777216 | tf_op jit(solution)/shard_map/broadcast_in_dim | solution.py:66
  270.7 5.9 all-to-all-start.3
  277.1 38.7 %fusion.2 = f32[2,8,32,128,128]{3,4,2,1,0:T(8,128)} fusion(f32[2,32,128,128]{3,2,1,0:T(8,128)S(1)} %convert_element_type.93, f32[8,32,128,128]{3,2,1,0:T(8,128)} %convert_element_type.81, f32[128,64]{0,1:T(8,128)S(1)} %get-tuple-element.54, f32[128,64]{0,1:T(8,128)S(1)} %get-tuple-element.53), kind=kOutput, calls=%fused_computation.2 | convolution fusion | flops 12893323264 | bytes 54591488 | tf_op jit(solution)/shard_map/dot_general | solution.py:55
  315.8 18.9 %fusion.47 = (f32[8,32,128,64]{2,3,1,0:T(8,128)}, f32[8,32,128,64]{2,3,1,0:T(8,128)}) fusion(f32[2,8,32,128,128]{3,4,2,1,0:T(8,128)} %fusion.2), kind=kLoop, calls=%fused_computation.48 | loop fusion | flops 4194304 | bytes 50331648 | tf_op jit(solution)/shard_map/sub | solution.py:60
  334.7 22.3 %fusion.35 = f32[8,32,128,128]{3,2,1,0:T(8,128)} fusion(f32[8,32,128,64]{2,3,1,0:T(8,128)} %get-tuple-element.14, f32[8,32,128,64]{2,3,1,0:T(8,128)} %get-tuple-element.13, f32[128,64]{0,1:T(8,128)S(1)} %get-tuple-element.52, f32[128,64]{0,1:T(8,128)S(1)} %get-tuple-element.51), kind=kOutput, calls=%fused_computation.34 | convolution fusion | flops 6446678016 | bytes 33619968 | tf_op jit(solution)/shard_map/yj,bxyc->bxjc/dot_general | solution.py:65
  357.0 19.2 %slice_subtract_fusion.2 = (f32[8,32,64,64]{3,2,1,0:T(8,128)}, f32[8,32,64,64]{3,2,1,0:T(8,128)}) fusion(f32[8,32,128,128]{3,2,1,0:T(8,128)} %fusion.35), kind=kLoop, calls=%fused_computation.44 | loop fusion | flops 2097152 | bytes 25165824 | tf_op jit(solution)/shard_map/sub | solution.py:68
  376.2 12.0 %maximum_bitcast_fusion.2 = f32[8,1,32,64,128]{4,3,2,0,1:T(8,128)} fusion(f32[8,32,64,64]{3,2,1,0:T(8,128)} %get-tuple-element.22, f32[8,32,64,64]{3,2,1,0:T(8,128)} %get-tuple-element.21), kind=kLoop, calls=%fused_computation.63 | loop fusion | flops 2097152 | bytes 16777216 | tf_op jit(solution)/shard_map/broadcast_in_dim | solution.py:66
  388.2 11.5 %copy.22 = f32[8,1,32,64,128]{4,2,0,1,3:T(8,128)} copy(f32[8,1,32,64,128]{4,3,2,0,1:T(8,128)} %maximum_bitcast_fusion.2) | data formatting | bytes 16777216 | tf_op jit(solution)/shard_map/broadcast_in_dim | solution.py:66
  399.7 59.7 %all-to-all-done.3 = f32[8,1,32,64,128]{4,2,0,1,3:T(8,128)} async-done(((f32[8,1,32,64,128]{4,2,0,1,3:T(8,128)}), f32[8,1,32,64,128]{4,2,0,1,3:T(8,128)}, u32[]{:S(2)}, u32[]{:S(2)}) %all-to-all-start.3) | async-done | bytes 8388640 | tf_op jit(solution)/shard_map/all_to_all | solution.py:76
  459.4 5.8 all-to-all-start.2
  465.8 38.8 %fusion.4 = f32[2,8,32,128,128]{3,4,2,1,0:T(8,128)} fusion(f32[2,32,128,128]{3,2,1,0:T(8,128)S(1)} %convert_element_type.91, f32[8,32,128,128]{3,2,1,0:T(8,128)} %convert_element_type.81, f32[128,64]{0,1:T(8,128)S(1)} %get-tuple-element.54, f32[128,64]{0,1:T(8,128)S(1)} %get-tuple-element.53), kind=kOutput, calls=%fused_computation.4 | convolution fusion | flops 12893323264 | bytes 54591488 | tf_op jit(solution)/shard_map/dot_general | solution.py:55
  504.6 18.9 %fusion.49 = (f32[8,32,128,64]{2,3,1,0:T(8,128)}, f32[8,32,128,64]{2,3,1,0:T(8,128)}) fusion(f32[2,8,32,128,128]{3,4,2,1,0:T(8,128)} %fusion.4), kind=kLoop, calls=%fused_computation.54 | loop fusion | flops 4194304 | bytes 50331648 | tf_op jit(solution)/shard_map/sub | solution.py:60
  523.4 22.3 %fusion.38 = f32[8,32,128,128]{3,2,1,0:T(8,128)} fusion(f32[8,32,128,64]{2,3,1,0:T(8,128)} %get-tuple-element.12, f32[8,32,128,64]{2,3,1,0:T(8,128)} %get-tuple-element.11, f32[128,64]{0,1:T(8,128)S(1)} %get-tuple-element.52, f32[128,64]{0,1:T(8,128)S(1)} %get-tuple-element.51), kind=kOutput, calls=%fused_computation.35 | convolution fusion | flops 6446678016 | bytes 33619968 | tf_op jit(solution)/shard_map/yj,bxyc->bxjc/dot_general | solution.py:65
  545.7 19.2 %slice_subtract_fusion.4 = (f32[8,32,64,64]{3,2,1,0:T(8,128)}, f32[8,32,64,64]{3,2,1,0:T(8,128)}) fusion(f32[8,32,128,128]{3,2,1,0:T(8,128)} %fusion.38), kind=kLoop, calls=%fused_computation.50 | loop fusion | flops 2097152 | bytes 25165824 | tf_op jit(solution)/shard_map/sub | solution.py:68
  564.9 12.0 %maximum_bitcast_fusion.1 = f32[8,1,32,64,128]{4,3,2,0,1:T(8,128)} fusion(f32[8,32,64,64]{3,2,1,0:T(8,128)} %get-tuple-element.20, f32[8,32,64,64]{3,2,1,0:T(8,128)} %get-tuple-element.19), kind=kLoop, calls=%fused_computation.62 | loop fusion | flops 2097152 | bytes 16777216 | tf_op jit(solution)/shard_map/broadcast_in_dim | solution.py:66
  576.9 11.5 %copy.19 = f32[8,1,32,64,128]{4,2,0,1,3:T(8,128)} copy(f32[8,1,32,64,128]{4,3,2,0,1:T(8,128)} %maximum_bitcast_fusion.1) | data formatting | bytes 16777216 | tf_op jit(solution)/shard_map/broadcast_in_dim | solution.py:66
  588.4 59.5 %all-to-all-done.2 = f32[8,1,32,64,128]{4,2,0,1,3:T(8,128)} async-done(((f32[8,1,32,64,128]{4,2,0,1,3:T(8,128)}), f32[8,1,32,64,128]{4,2,0,1,3:T(8,128)}, u32[]{:S(2)}, u32[]{:S(2)}) %all-to-all-start.2) | async-done | bytes 8388640 | tf_op jit(solution)/shard_map/all_to_all | solution.py:76
  647.8 5.8 all-to-all-start.1
  654.2 38.7 %fusion.6 = f32[2,8,32,128,128]{3,4,2,1,0:T(8,128)} fusion(f32[2,32,128,128]{3,2,1,0:T(8,128)S(1)} %convert_element_type.83, f32[8,32,128,128]{3,2,1,0:T(8,128)} %convert_element_type.81, f32[128,64]{0,1:T(8,128)S(1)} %get-tuple-element.54, f32[128,64]{0,1:T(8,128)S(1)} %get-tuple-element.53), kind=kOutput, calls=%fused_computation.6 | convolution fusion | flops 12893323264 | bytes 54591488 | tf_op jit(solution)/shard_map/dot_general | solution.py:55
  692.9 18.9 %fusion.51 = (f32[8,32,128,64]{2,3,1,0:T(8,128)}, f32[8,32,128,64]{2,3,1,0:T(8,128)}) fusion(f32[2,8,32,128,128]{3,4,2,1,0:T(8,128)} %fusion.6), kind=kLoop, calls=%fused_computation.60 | loop fusion | flops 4194304 | bytes 50331648 | tf_op jit(solution)/shard_map/sub | solution.py:60
  711.8 22.5 %fusion.41 = f32[8,32,128,128]{3,2,1,0:T(8,128)} fusion(f32[8,32,128,64]{2,3,1,0:T(8,128)} %get-tuple-element.10, f32[8,32,128,64]{2,3,1,0:T(8,128)} %get-tuple-element.9, f32[128,64]{0,1:T(8,128)S(1)} %get-tuple-element.52, f32[128,64]{0,1:T(8,128)S(1)} %get-tuple-element.51), kind=kOutput, calls=%fused_computation.36 | convolution fusion | flops 6446678016 | bytes 33619968 | tf_op jit(solution)/shard_map/yj,bxyc->bxjc/dot_general | solution.py:65
  734.2 19.2 %slice_subtract_fusion.6 = (f32[8,32,64,64]{3,2,1,0:T(8,128)}, f32[8,32,64,64]{3,2,1,0:T(8,128)}) fusion(f32[8,32,128,128]{3,2,1,0:T(8,128)} %fusion.41), kind=kLoop, calls=%fused_computation.56 | loop fusion | flops 2097152 | bytes 25165824 | tf_op jit(solution)/shard_map/sub | solution.py:68
  753.4 12.1 %maximum_bitcast_fusion = f32[8,1,32,64,128]{4,3,2,0,1:T(8,128)} fusion(f32[8,32,64,64]{3,2,1,0:T(8,128)} %get-tuple-element.18, f32[8,32,64,64]{3,2,1,0:T(8,128)} %get-tuple-element.17), kind=kLoop, calls=%fused_computation.61 | loop fusion | flops 2097152 | bytes 16777216 | tf_op jit(solution)/shard_map/broadcast_in_dim | solution.py:66
  765.5 11.5 %copy.16 = f32[8,1,32,64,128]{4,2,0,1,3:T(8,128)} copy(f32[8,1,32,64,128]{4,3,2,0,1:T(8,128)} %maximum_bitcast_fusion) | data formatting | bytes 16777216 | tf_op jit(solution)/shard_map/broadcast_in_dim | solution.py:66
  777.0 59.2 %all-to-all-done.1 = f32[8,1,32,64,128]{4,2,0,1,3:T(8,128)} async-done(((f32[8,1,32,64,128]{4,2,0,1,3:T(8,128)}), f32[8,1,32,64,128]{4,2,0,1,3:T(8,128)}, u32[]{:S(2)}, u32[]{:S(2)}) %all-to-all-start.1) | async-done | bytes 8388640 | tf_op jit(solution)/shard_map/all_to_all | solution.py:76
  836.2 5.8 all-to-all-start
  842.7 4.4 copy.26
  847.1 4.4 copy.23
  851.5 8.2 copy.20
  859.7 9.9 convolution_bitcast_fusion
  869.6 9.8 convolution_bitcast_fusion.1
  879.3 10.1 convolution_bitcast_fusion.2
  889.4 135.2 %all-to-all-done = f32[8,1,32,64,128]{4,2,0,1,3:T(8,128)} async-done(((f32[8,1,32,64,128]{4,2,0,1,3:T(8,128)}), f32[8,1,32,64,128]{4,2,0,1,3:T(8,128)}, u32[]{:S(2)}, u32[]{:S(2)}) %all-to-all-start) | async-done | bytes 8388640 | tf_op jit(solution)/shard_map/all_to_all | solution.py:76
  1024.6 4.4 copy.17
  1029.0 9.9 convolution_bitcast_fusion.3
  1038.9 33.3 %fusion.60 = (f32[8,1,64,16,64]{4,2,3,0,1:T(8,128)S(1)}, f32[8,1,64,16,64]{4,2,3,0,1:T(8,128)}, f32[8,1,64,16,64]{4,2,3,0,1:T(8,128)}, f32[8,1,64,16,64]{4,2,3,0...) fusion(f32[8,1,128,16,128]{4,2,3,0,1:T(8,128)} %convolution_bit, ...), kind=kLoop, calls=%fused_computation.82 | loop fusion | flops 9961472 | bytes 50593824 | tf_op jit(solution)/shard_map/mul | solution.py:86
  1072.3 13.7 %maximum_maximum_fusion = f32[8,4,64,16,128]{4,2,3,0,1:T(8,128)S(1)} fusion(f32[8,1,64,16,64]{4,2,3,0,1:T(8,128)} %get-tuple-element.41, f32[8,1,64,16,64]{4,2,3,0,1:T(8,128)} %get-tuple-element.42, f32[8,1,64,16,64]{4,2,3,0,1:T(8,128)} %get-tuple-element.39, f32[8,1,64,16,64]{4,2,3,0,1:T(8,128)} %get-tuple-element.40, ...), kind=kLoop, calls=%fused_computation.24 | loop fusion | flops 29360128 | bytes 33554432 | tf_op jit(solution)/shard_map/concatenate | solution.py:88
  1086.0 11.6 %copy.27 = f32[8,4,64,16,128]{4,3,2,1,0:T(8,128)} copy(f32[8,4,64,16,128]{4,2,3,0,1:T(8,128)S(1)} %maximum_maximum_fusion) | data formatting | bytes 33554432 | tf_op jit(solution)/shard_map/concatenate | solution.py:88
  (34 shorter events, 3.1 us)
Async XLA Ops:
  6.5 139.3 %all-reduce.3.cloned.1.call-start = ((), (), s32[]{:S(2)}) async-start(), calls=%async_computation.4 | async-start | bytes 16777216 | tf_op jit(solution)/shard_map/psum | solution.py:13
  15.5 11.9 %copy-start.3 = (s32[3,64]{1,0:T(4,128)S(1)}, s32[3,64]{1,0:T(4,128)}, u32[]{:S(2)}) copy-start(s32[3,64]{1,0:T(4,128)} %param.8) | copy-start | bytes 2308
  270.6 5.9 copy-start.2
  270.7 188.8 %all-to-all-start.3 = ((f32[8,1,32,64,128]{4,2,0,1,3:T(8,128)}), f32[8,1,32,64,128]{4,2,0,1,3:T(8,128)}, u32[]{:S(2)}, u32[]{:S(2)}) async-start(f32[8,1,32,64,128]{4,2,0,1,3:T(8,128)} %copy.25), calls=%async_computation.3 | async-start | bytes 16777216 | tf_op jit(solution)/shard_map/all_to_all | solution.py:76
  399.7 65.6 %copy-start.1 = (bf16[2,32,128,128]{3,2,1,0:T(8,128)(2,1)S(1)}, bf16[2,32,128,128]{3,2,1,0:T(8,128)(2,1)}, u32[]{:S(2)}) copy-start(bf16[2,32,128,128]{3,2,1,0:T(8,128)(2,1)} %get-tuple-element.7) | copy-start | bytes 6291460
  459.4 188.4 %all-to-all-start.2 = ((f32[8,1,32,64,128]{4,2,0,1,3:T(8,128)}), f32[8,1,32,64,128]{4,2,0,1,3:T(8,128)}, u32[]{:S(2)}, u32[]{:S(2)}) async-start(f32[8,1,32,64,128]{4,2,0,1,3:T(8,128)} %copy.22), calls=%async_computation.2 | async-start | bytes 16777216 | tf_op jit(solution)/shard_map/all_to_all | solution.py:76
  588.4 65.2 %copy-start = (bf16[2,32,128,128]{3,2,1,0:T(8,128)(2,1)S(1)}, bf16[2,32,128,128]{3,2,1,0:T(8,128)(2,1)}, u32[]{:S(2)}) copy-start(bf16[2,32,128,128]{3,2,1,0:T(8,128)(2,1)} %get-tuple-element.8) | copy-start | bytes 6291460
  647.8 188.4 %all-to-all-start.1 = ((f32[8,1,32,64,128]{4,2,0,1,3:T(8,128)}), f32[8,1,32,64,128]{4,2,0,1,3:T(8,128)}, u32[]{:S(2)}, u32[]{:S(2)}) async-start(f32[8,1,32,64,128]{4,2,0,1,3:T(8,128)} %copy.19), calls=%async_computation.1 | async-start | bytes 16777216 | tf_op jit(solution)/shard_map/all_to_all | solution.py:76
  777.0 65.1 %copy-start.6 = (s32[1,64]{1,0:T(1,128)S(1)}, s32[1,64]{1,0:T(1,128)}, u32[]{:S(2)}) copy-start(s32[1,64]{1,0:T(1,128)} %get-tuple-element.45) | copy-start | bytes 772
  777.0 65.2 %copy-start.4 = (s32[3,64]{1,0:T(4,128)S(1)}, s32[3,64]{1,0:T(4,128)}, u32[]{:S(2)}) copy-start(s32[3,64]{1,0:T(4,128)} %param.8) | copy-start | bytes 2308
  777.0 65.3 %copy-start.5 = (s32[64]{0:T(128)S(1)}, s32[64]{0:T(128)}, u32[]{:S(2)}) copy-start(s32[64]{0:T(128)} %get-tuple-element.48) | copy-start | bytes 772
  836.2 188.4 %all-to-all-start = ((f32[8,1,32,64,128]{4,2,0,1,3:T(8,128)}), f32[8,1,32,64,128]{4,2,0,1,3:T(8,128)}, u32[]{:S(2)}, u32[]{:S(2)}) async-start(f32[8,1,32,64,128]{4,2,0,1,3:T(8,128)} %copy.16), calls=%async_computation | async-start | bytes 16777216 | tf_op jit(solution)/shard_map/all_to_all | solution.py:76
  859.7 19.6 %slice-start = ((s8[8388608]{0:T(1024)(128)(4,1)}), s8[4194304]{0:T(1024)(128)(4,1)S(1)}, s32[]{:S(2)}) async-start(s8[8388608]{0:T(1024)(128)(4,1)} %bitcast.118), calls=%async_computation.5 | async-start | bytes 8388608
  869.6 9.8 slice-start.1
  1029.0 9.9 copy-start.7
Sparse Core Ops, SparseCore 0:
  15.6 130.2 all-reduce.2
where the time goes:
time: 1110 us; the launch traced here: 1100 us
  waiting for transfers between devices  431 us (39%)
  matrix products  284 us (26%)
  other arithmetic  269 us (24%)
  local copies, waits for them, and re-layouts  80.9 us (7%)
  starting transfers between devices  23.4 us (2%)
  between operations  16.4 us (1%)
    all_to_all x4, waiting for transfers between devices, per_device(): lax.all_to_all(planes, 'plane', split_axis=3, concat_axis=2, tiled=True)  314 us
    dot_general x4, matrix products, per_device(): jnp.dot(product.reshape(-1, length), table_z, precision=highest)  155 us
    psum x1, waiting for transfers between devices, broadcast(): return lax.psum(block, axis)  118 us
    dot_general x4, matrix products, per_device(): along_y = jnp.einsum('yj,bxyc->bxjc', table_y, mixed_z, precision=highest)  89.4 us
    sub x4, other arithmetic, per_device(): along_y[:, :, :kept_count, :kept_count]  76.8 us
    sub x4, other arithmetic, per_device(): along_z[0, ..., :kept_count] - along_z[1, ..., kept_count:]  75.5 us
    broadcast_in_dim x4, other arithmetic, per_device(): jnp.concatenate([along_y[:, :, :kept_count, :kept_count] - along_y[:, :,...  48 us
    broadcast_in_dim x4, local copies, waits for them, and re-layouts, per_device(): jnp.concatenate([along_y[:, :, :kept_count, :kept_count] - along_y[:, :,...  45.9 us
  transfers between devices with their start and end apart: 5, of which 5 were waited for; matrix products, arithmetic and copies ran while one was open for 39% of the time, Pallas kernels for 0%

commit v1 on v0

v1 whole, which is shorter than its diff:
```python
import functools
import math

import jax
import jax.numpy as jnp
from jax import lax
from jax.experimental import pallas as pl
from jax.experimental.pallas import tpu as pltpu
from jax.sharding import PartitionSpec as P

kinetic_coef = 0.5 * (2.0 * math.pi / 64.0) ** 2
code_top = 32700.0
code_steps = 256.0 / math.log(2.0)
vmem_limit = 56 * 1024 * 1024
f32 = jnp.float32
bf16 = jnp.bfloat16


def angle_table(frequency, position, length):
    phase_index = position[:, None] * frequency[None, :] % length
    angles = phase_index.astype(f32) * (2.0 * math.pi / length)
    norm_factor = 1.0 / math.sqrt(length)
    return jnp.cos(angles) * norm_factor, -jnp.sin(angles) * norm_factor


def signed_square(frequency, length):
    signed = jnp.where(frequency < length // 2, frequency, frequency - length).astype(f32)
    return signed * signed


def split_table(value):
    high = lax.reduce_precision(value, 8, 7)
    return high.astype(bf16), (value - high).astype(bf16)


def split_pair(value):
    high = value.astype(bf16)
    low = (value - high.astype(f32)).astype(bf16)
    return high, low


def left_table(frequency, position, length):
    cos, sin = angle_table(frequency, position, length)
    high, low = split_table(jnp.concatenate([cos, sin], axis=1).T)
    top = jnp.concatenate([high, high], axis=1)
    bottom = jnp.concatenate([low, jnp.zeros_like(low)], axis=1)
    return jnp.concatenate([top, bottom], axis=0)


def right_table(frequency, position, length):
    cos, sin = angle_table(frequency, position, length)
    table = jnp.concatenate(
        [jnp.concatenate([cos, sin], axis=1), jnp.concatenate([-sin, cos], axis=1)], axis=0
    )
    return jnp.concatenate(split_table(table), axis=1)


def left_dot(table, planes, keep):
    stacked = jnp.concatenate(
        [jnp.concatenate(split_pair(plane), axis=0) for plane in planes], axis=1
    )
    sums = jnp.dot(table, stacked, preferred_element_type=f32)
    half = 2 * keep
    sums = sums[:half] + sums[half:]
    lane = lax.broadcasted_iota(jnp.int32, (keep, half), 1)
    results = []
    for index in range(len(planes)):
        part = sums[:, index * half : (index + 1) * half]
        turned = pltpu.roll(part[keep:], keep, 1)
        results.append(part[:keep] + jnp.where(lane < keep, -turned, turned))
    return results


def forward_kernel(
    slots, planes_total, step_planes, keep, columns, patterns, parts,
    source_ref, target_ref, orbital_ref, wz_ref, ty_ref, *rest
):
    potential_refs = rest[:slots]
    out_refs = rest[slots : slots + parts]
    potential, held, semaphore = rest[slots + parts :]
    band, step = pl.program_id(0), pl.program_id(1)

    @pl.when((band == 0) & (step == 0))
    def _():
        def fetch(block, pattern):
            return pltpu.make_async_copy(block, potential.at[pattern], semaphore.at[pattern])

        gathered = slots == 1
        for pattern in range(patterns):
            if gathered:
                fetch(potential_refs[0].at[source_ref[pattern]], pattern).start()
            for slot in range(0 if gathered else slots):

                @pl.when(source_ref[pattern] == slot)
                def _():
                    fetch(potential_refs[slot], pattern).start()

        for pattern in range(patterns):
            fetch(potential_refs[0].at[0] if gathered else potential_refs[0], pattern).wait()

    def one_plane(index, carry):
        at = step * step_planes + index
        orbital = orbital_ref[0, index].astype(f32)
        highs, lows = [], []
        for pattern in range(patterns):
            split = [
                split_pair(orbital * potential[pattern, part, at].astype(f32)) for part in range(2)
            ]
            highs.append(jnp.concatenate([split[0][0], split[1][0]], axis=1))
            lows.append(jnp.concatenate([split[0][1], split[1][1]], axis=1))
        half = 2 * keep
        high_sum = jnp.dot(
            jnp.concatenate(highs, axis=0), wz_ref[...], preferred_element_type=f32
        )
        low_sum = jnp.dot(
            jnp.concatenate(lows, axis=0), wz_ref[:, :half], preferred_element_type=f32
        )
        along_z = high_sum[:, :half] + high_sum[:, half:] + low_sum
        length = orbital.shape[0]
        for pair in range(patterns // 2):
            first = 2 * pair
            results = left_dot(
                ty_ref[...],
                [along_z[p * length : (p + 1) * length] for p in (first, first + 1)],
                keep,
            )
            for offset, result in enumerate(results):
                for part in range(parts):
                    held[first + offset, at, part] = result[part * columns : (part + 1) * columns]
        return carry

    lax.fori_loop(0, step_planes, one_plane, 0, unroll=math.gcd(step_planes, 4))

    @pl.when(step == pl.num_programs(1) - 1)
    def _():
        rows = planes_total * columns
        for shift in range(parts):
            target = target_ref[shift]
            out_ref = out_refs[shift]
            for pair in range(patterns // 2):
                inverse = []
                for pattern in (2 * pair, 2 * pair + 1):
                    top = jnp.zeros((columns, 2 * keep), f32)
                    for at in range(planes_total):
                        top = jnp.maximum(top, jnp.abs(held[pattern, at, target]))
                    top = jnp.max(top, axis=0, keepdims=True)
                    code = jnp.ceil(
                        jnp.log(jnp.maximum(top, 1e-30) * (1.0 / code_top)) * code_steps
                    )
                    inverse.append(jnp.exp(code * (-1.0 / code_steps)))
                    row = (patterns // 2) * rows + pattern
                    out_ref[0, row : row + 1, :] = code.astype(jnp.int32)
                for at in range(planes_total):
                    low, high = [
                        jnp.round(held[2 * pair + which, at, target] * inverse[which]).astype(
                            jnp.int32
                        )
                        for which in range(2)
                    ]
                    row = pair * rows + at * columns
                    out_ref[0, row : row + columns, :] = (high << 16) | (low & 0xFFFF)


def forward(
    orbitals, potentials, source, targets, wz, ty, first_plane, planes, step_planes, first_band,
    bands, keep, patterns
):
    parts = targets.shape[0]
    columns = keep // parts
    length = orbitals.shape[2]
    slots = len(potentials)
    rows = (patterns // 2) * planes * columns + 8
    kernel = functools.partial(
        forward_kernel, slots, planes, step_planes, keep, columns, patterns, parts
    )
    whole = pl.BlockSpec(memory_space=pl.ANY)
    fixed = lambda array: pl.BlockSpec(array.shape, lambda b, g, *_: (0,) * array.ndim)
    flops = 16 * bands * planes * patterns * length * length * 2 * keep
    return pl.pallas_call(
        kernel,
        grid_spec=pltpu.PrefetchScalarGridSpec(
            num_scalar_prefetch=2,
            grid=(bands, planes // step_planes),
            in_specs=[
                pl.BlockSpec(
                    (1, step_planes, length, length),
                    lambda b, g, *_: (b + first_band, g + first_plane // step_planes, 0, 0),
                ),
                fixed(wz),
                fixed(ty),
            ]
            + [whole] * slots,
            out_specs=[pl.BlockSpec((1, rows, 2 * keep), lambda b, g, *_: (b, 0, 0))] * parts,
            scratch_shapes=[
                pltpu.VMEM((patterns, 2, planes, length, length), bf16),
                pltpu.VMEM((patterns, planes, parts, columns, 2 * keep), f32),
                pltpu.SemaphoreType.DMA((patterns,)),
            ],
        ),
        out_shape=[jax.ShapeDtypeStruct((bands, rows, 2 * keep), jnp.int32)] * parts,
        compiler_params=pltpu.CompilerParams(
            dimension_semantics=("arbitrary", "arbitrary"), vmem_limit_bytes=vmem_limit
        ),
        cost_estimate=pl.CostEstimate(
            flops=flops, bytes_accessed=2 * bands * planes * length * length, transcendentals=0
        ),
        name="forward_zy",
    )(source, targets, orbitals, wz, ty, *potentials)


def final_kernel(
    plane_counts, first_band, keep, columns, patterns, parts, chained,
    ky_ref, energy_ref, tx_ref, kinetic_ref, *rest
):
    count = len(plane_counts) * parts
    chunk_refs = rest[:count]
    out_ref, wide = rest[count + chained :]
    energy = energy_ref[pl.program_id(0) + first_band]
    total = parts * sum(plane_counts)
    for pair in range(patterns // 2):
        base = 0
        for chunk, planes in enumerate(plane_counts):
            rows = planes * columns
            for shift in range(parts):
                ref = chunk_refs[chunk * parts + shift]
                scales = []
                for pattern in (2 * pair, 2 * pair + 1):
                    row = (patterns // 2) * rows + pattern
                    scales.append(jnp.exp(ref[0, row : row + 1, :].astype(f32) * (1.0 / code_steps)))
                words = ref[0, pair * rows : (pair + 1) * rows, :]
                wide[0, base : base + rows, :] = ((words << 16) >> 16).astype(f32) * scales[0]
                wide[1, base : base + rows, :] = (words >> 16).astype(f32) * scales[1]
                base += rows

        def two_columns(index, carry):
            for which in range(2):
                column = [2 * index, 2 * index + 1]
                results = left_dot(
                    tx_ref[...],
                    [wide[which, pl.ds(j, total, stride=columns), :] for j in column],
                    keep,
                )
                for j, result in zip(column, results):
                    kinetic = kinetic_ref[...] + ky_ref[j]
                    out_ref[0, 2 * pair + which, pl.ds(j, keep, stride=columns), :] = (
                        result * (1.0 / (1.0 + kinetic / energy))
                    )
            return carry

        lax.fori_loop(0, columns // 2, two_columns, 0, unroll=math.gcd(columns // 2, 4))


def final(chunks, plane_counts, band_offsets, first_band, bands, held_out, ky, energy, tx, kinetic, patterns, keep, all_bands):
    parts = len(chunks[0])
    columns = keep // parts
    total = parts * sum(plane_counts)
    chained = 0 if held_out is None else 1
    kernel = functools.partial(
        final_kernel, plane_counts, first_band, keep, columns, patterns, parts, chained
    )
    fixed = lambda array: pl.BlockSpec(array.shape, lambda b, *_: (0,) * array.ndim)
    chunk_specs = []
    for arrays, offset in zip(chunks, band_offsets):
        for array in arrays:
            chunk_specs.append(
                pl.BlockSpec((1,) + array.shape[1:], lambda b, *_, o=offset: (b + o, 0, 0))
            )
    flat = [array for arrays in chunks for array in arrays]
    out_block = (1, patterns, keep * columns, 2 * keep)
    operands = [ky, energy, tx, kinetic] + flat
    if chained:
        operands.append(held_out)
    return pl.pallas_call(
        kernel,
        grid_spec=pltpu.PrefetchScalarGridSpec(
            num_scalar_prefetch=2,
            grid=(bands,),
            in_specs=[fixed(tx), fixed(kinetic)]
            + chunk_specs
            + [pl.BlockSpec(memory_space=pl.ANY)] * chained,
            out_specs=pl.BlockSpec(out_block, lambda b, *_: (b + first_band, 0, 0, 0)),
            scratch_shapes=[pltpu.VMEM((2, total * columns, 2 * keep), f32)],
        ),
        out_shape=jax.ShapeDtypeStruct((all_bands,) + out_block[1:], f32),
        input_output_aliases={len(operands) - 1: 0} if chained else {},
        compiler_params=pltpu.CompilerParams(
            dimension_semantics=("arbitrary",), vmem_limit_bytes=vmem_limit
        ),
        cost_estimate=pl.CostEstimate(
            flops=16 * bands * patterns * columns * total * 2 * keep * 2 * keep,
            bytes_accessed=6 * bands * patterns * keep * columns * 2 * keep,
            transcendentals=0,
        ),
        name="final_x",
    )(*operands)


def permute(array, axis, step):
    return lax.ppermute(array, axis, [(i, i ^ step) for i in range(lax.axis_size(axis))])


def gather_chips(block):
    return [block] + [permute(block, "band", step) for step in range(2, lax.axis_size("band"), 2)]


def gather_cores(blocks):
    others = [permute(block, "band", 1) for block in blocks]
    return [block for pair in zip(blocks, others) for block in pair]


def cut(bands):
    sizes = [2] * ((bands - 1) // 2)
    sizes += [1] * (bands - sum(sizes))
    return [(sum(sizes[:index]), size) for index, size in enumerate(sizes)]


def halves(bands):
    middle = (bands + 1) // 2
    return [(0, middle), (middle, bands - middle)] if bands > 1 else [(0, bands)]


def holder(groups, first):
    for index, (start, count) in enumerate(groups):
        if start <= first < start + count:
            return index, first - start


def per_device(orbitals, potential_slots, pattern_owner, retained, band_energy):
    bands, local_planes, length, _ = orbitals.shape
    keep = retained.shape[1]
    patterns = pattern_owner.shape[0]
    parts = lax.axis_size("plane")
    rank = lax.axis_index("plane")
    columns = keep // parts

    ends = [max(1, local_planes // 8), max(2, local_planes * 3 // 8), local_planes]
    chunks = [
        (start, end - start, math.gcd(start, end - start)) for start, end in zip([0] + ends, ends)
    ]
    band_rank = lax.axis_index("band")
    sources = rank ^ jnp.arange(parts, dtype=jnp.int32)
    blocks = [
        lax.slice_in_dim(potential_slots[0], start, start + planes, axis=1)
        for start, planes, _ in chunks
    ]
    potentials = [(gather_cores(gather_chips(blocks[0])), band_rank ^ pattern_owner)]
    potentials += [([lax.all_gather(block, "band")], pattern_owner) for block in blocks[1:]]

    position = jnp.arange(length, dtype=jnp.int32)
    wz = right_table(retained[2], position, length)
    ty = left_table(retained[1], position, length)
    plane_order = jnp.concatenate(
        [
            (sources[:, None] * local_planes + start + jnp.arange(planes, dtype=jnp.int32)).reshape(-1)
            for start, planes, _ in chunks
        ]
    )
    tx = left_table(retained[0], plane_order, length)
    ky_local = lax.dynamic_slice_in_dim(retained[1], rank * columns, columns)
    kz = signed_square(retained[2], length)
    kinetic = kinetic_coef * (
        signed_square(retained[0], length)[:, None] + jnp.concatenate([kz, kz])[None, :]
    )
    ky = kinetic_coef * signed_square(ky_local, length)

    def run(chunk, first, count):
        start, planes, step_planes = chunks[chunk]
        slots, source = potentials[chunk]
        made = forward(
            orbitals, slots, source, sources, wz, ty, start, planes, step_planes,
            first, count, keep, patterns
        )
        return [made[0]] + [permute(made[s], "plane", s) for s in range(1, parts)]

    groups = [halves(bands)] * (len(chunks) - 1) + [cut(bands)]
    received = [
        [run(chunk, first, count) for first, count in groups[chunk]] for chunk in range(len(chunks))
    ]
    out = None
    for first, count in groups[-1]:
        places = [holder(chunk_groups, first) for chunk_groups in groups]
        out = final(
            [received[chunk][index] for chunk, (index, _) in enumerate(places)],
            [planes for _, planes, _ in chunks],
            [offset for _, offset in places],
            first, count, out, ky, band_energy, tx, kinetic, patterns, keep, bands,
        )
    return out.reshape(bands, patterns, keep, columns, 2 * keep)


def solution(mesh):
    in_specs = (
        P("band", "plane", None, None),
        P("band", None, "plane", None, None),
        P(),
        P(),
        P("band"),
    )
    out_specs = P("band", None, None, "plane", None)
    return jax.shard_map(
        per_device, mesh=mesh, in_specs=in_specs, out_specs=out_specs, check_vma=False
    )
```

time: 1110 us -> 443 us (0.40)
  waiting for transfers between devices: 431 us -> 140 us
  matrix products: 284 us -> 0 us
  other arithmetic: 269 us -> 6.18 us
  Pallas kernels: 0 us -> 204 us
  local copies, waits for them, and re-layouts: 80.9 us -> 10.5 us
  starting transfers between devices: 23.4 us -> 64.3 us
    all_to_all x4 -> x0, waiting for transfers between devices: 314 us -> none  [per_device(): lax.all_to_all(planes, 'plane', split_axis=3, concat_axis=2, tiled=True)]
    dot_general x12 -> x0, matrix products: 284 us -> none  [the longest x4 155 us: per_device(): jnp.dot(product.reshape(-1, length), table_z, precision=highest)]
    pallas_call x0 -> x14, Pallas kernels: none -> 204 us  [the longest x9 157 us: forward(): pl.pallas_call(kernel, grid_spec=pltpu.PrefetchScalarGridSpec(num_scalar_...]
    sub x8 -> x0, other arithmetic: 152 us -> none  [the longest x4 76.8 us: per_device(): along_y[:, :, :kept_count, :kept_count]]
    ppermute x0 -> x34, waiting for transfers between devices: none -> 133 us  [permute(): lax.ppermute(array, axis, [(i, i ^ step) for i in range(lax.axis_size(axi...]
    psum x1 -> x0, waiting for transfers between devices: 118 us -> none  [broadcast(): return lax.psum(block, axis)]
    ppermute x0 -> x34, starting transfers between devices: none -> 64.2 us  [permute(): lax.ppermute(array, axis, [(i, i ^ step) for i in range(lax.axis_size(axi...]
    broadcast_in_dim x4 -> x0, other arithmetic: 48 us -> none  [per_device(): jnp.concatenate([along_y[:, :, :kept_count, :kept_count] - along_y[:, :,...]
  transfers between devices with their start and end apart: 5 -> 36, of which waited for: 5 -> 9; matrix products, arithmetic and copies ran while one was open for 39% -> 3% of each run, Pallas kernels for 0% -> 45%
where the time goes in v1:
time: 443 us; the launch traced here: 438 us
  Pallas kernels  204 us (46%)
  waiting for transfers between devices  140 us (32%)
  starting transfers between devices  64.3 us (15%)
  between operations  14 us (3%)
  local copies, waits for them, and re-layouts  10.5 us (2%)
  other arithmetic  6.18 us (1%)
    pallas_call x9, Pallas kernels, forward(): pl.pallas_call(kernel, grid_spec=pltpu.PrefetchScalarGridSpec(num_scalar_...  157 us
    ppermute x34, waiting for transfers between devices, permute(): lax.ppermute(array, axis, [(i, i ^ step) for i in range(lax.axis_size(axi...  133 us
    ppermute x34, starting transfers between devices, permute(): lax.ppermute(array, axis, [(i, i ^ step) for i in range(lax.axis_size(axi...  64.2 us
    pallas_call x5, Pallas kernels, final(): pl.pallas_call(kernel, grid_spec=pltpu.PrefetchScalarGridSpec(num_scalar_...  46.8 us
  transfers between devices with their start and end apart: 36, of which 9 were waited for; matrix products, arithmetic and copies ran while one was open for 3% of the time, Pallas kernels for 45%

profile of v1, /device:TPU:0, one launch (start us, length us, event | category | flops | bytes accessed | tf_op | source)
XLA Modules:
  0.0 438.1 jit_solution(16130243963633281339)
XLA Ops:
  6.5 1.9 slice.28
  8.5 2.5 slice.29
  11.1 1.0 slice.27.rest_0_
  12.1 4.0 collective-permute-start.5
  17.8 0.8 slice_bitcast_fusion.2
  20.6 0.8 fusion.27
  21.5 1.2 broadcast_xor_fusion.source_ref
  22.6 2.7 collective-permute-done.5.rest_6_
  25.3 7.8 %collective-permute-done.3.rest_4_ = bf16[2,4,128,128]{3,2,1,0:T(8,128)(2,1)S(1)} collective-permute-done((bf16[2,4,128,128]{3,2,1,0:T(8,128)(2,1)S(1)}, bf16[2,4,128,128]{3,2,1,0:T(8,128)(2,1)S(1)}, u32[]{:S(2)}, u32[]{:S(2)}) %collective-permute-start.3) | collective-permute-done | bytes 262176 | tf_op jit(solution)/shard_map/ppermute | solution.py:299
  34.5 0.7 copy.19.wz_ref
  36.8 0.7 copy-done.19
  37.5 11.1 %forward_zy.14 = (s32[4,136,128]{2,1,0:T(8,128)}, s32[4,136,128]{2,1,0:T(8,128)}, s32[4,136,128]{2,1,0:T(8,128)}, s32[4,136,128]{2,1,0:T(8,128)}) custom-call(s32[4]{0:T(128)} %broadcast_xor_fusion.source_ref, s32[4]{0:T(128)} %iota_xor_fusion.target_ref, bf16[8,32,128,128]{3,2,1,0:T(8,128)(2,1)} %orbital_ref.17, bf16[256,256]{1,0:T(8,128)(2,1)} %copy.19.wz_ref, ...), custom_call_target="tpu_custom_call" | custom-call | flops 2147483648 | bytes 524288 | tf_op jit(solution)/shard_map/forward_zy/pallas_call | solution.py:179
  48.6 1.5 collective-permute-start.22
  50.1 2.7 collective-permute-start.23
  53.1 10.8 %forward_zy.9 = (s32[4,136,128]{2,1,0:T(8,128)}, s32[4,136,128]{2,1,0:T(8,128)}, s32[4,136,128]{2,1,0:T(8,128)}, s32[4,136,128]{2,1,0:T(8,128)}) custom-call(s32[4]{0:T(128)} %broadcast_xor_fusion.source_ref, s32[4]{0:T(128)} %iota_xor_fusion.target_ref, bf16[8,32,128,128]{3,2,1,0:T(8,128)(2,1)} %orbital_ref.17, bf16[256,256]{1,0:T(8,128)(2,1)} %copy.19.wz_ref, ...), custom_call_target="tpu_custom_call" | custom-call | flops 2147483648 | bytes 524288 | tf_op jit(solution)/shard_map/forward_zy/pallas_call | solution.py:179
  64.5 3.6 collective-permute-start.8
  68.1 18.4 %forward_zy.15 = (s32[4,264,128]{2,1,0:T(8,128)}, s32[4,264,128]{2,1,0:T(8,128)}, s32[4,264,128]{2,1,0:T(8,128)}, s32[4,264,128]{2,1,0:T(8,128)}) custom-call(s32[4]{0:T(128)} %source_ref.13, s32[4]{0:T(128)} %iota_xor_fusion.target_ref, bf16[8,32,128,128]{3,2,1,0:T(8,128)(2,1)} %orbital_ref.17, bf16[256,256]{1,0:T(8,128)(2,1)} %copy.19.wz_ref, ...), custom_call_target="tpu_custom_call" | custom-call | flops 4294967296 | bytes 1048576 | tf_op jit(solution)/shard_map/forward_zy/pallas_call | solution.py:179
  87.3 18.6 %forward_zy.10 = (s32[4,264,128]{2,1,0:T(8,128)}, s32[4,264,128]{2,1,0:T(8,128)}, s32[4,264,128]{2,1,0:T(8,128)}, s32[4,264,128]{2,1,0:T(8,128)}) custom-call(s32[4]{0:T(128)} %source_ref.13, s32[4]{0:T(128)} %iota_xor_fusion.target_ref, bf16[8,32,128,128]{3,2,1,0:T(8,128)(2,1)} %orbital_ref.17, bf16[256,256]{1,0:T(8,128)(2,1)} %copy.19.wz_ref, ...), custom_call_target="tpu_custom_call" | custom-call | flops 4294967296 | bytes 1048576 | tf_op jit(solution)/shard_map/forward_zy/pallas_call | solution.py:179
  105.9 3.6 collective-permute-start.26
  110.3 3.8 collective-permute-start.11
  114.1 6.1 %all-gather.7.cloned.1.call-done = bf16[16,20,128,128]{3,2,1,0:T(8,128)(2,1)} async-done(((bf16[2,20,128,128]{3,2,1,0:T(8,128)(2,1)}), bf16[16,20,128,128]{3,2,1,0:T(8,128)(2,1)}) %all-gather.7.cloned.1.call-update) | async-done | bytes 10485776 | tf_op jit(solution)/shard_map/all_gather | solution.py:347
  120.2 23.2 %forward_zy.17 = (s32[2,648,128]{2,1,0:T(8,128)}, s32[2,648,128]{2,1,0:T(8,128)}, s32[2,648,128]{2,1,0:T(8,128)}, s32[2,648,128]{2,1,0:T(8,128)}) custom-call(s32[4]{0:T(128)} %source_ref.13, s32[4]{0:T(128)} %iota_xor_fusion.target_ref, bf16[8,32,128,128]{3,2,1,0:T(8,128)(2,1)} %orbital_ref.17, bf16[256,256]{1,0:T(8,128)(2,1)} %copy.19.wz_ref, ...), custom_call_target="tpu_custom_call" | custom-call | flops 5368709120 | bytes 1310720 | tf_op jit(solution)/shard_map/forward_zy/pallas_call | solution.py:179
  143.4 1.5 collective-permute-start.31
  144.9 23.1 %forward_zy.16 = (s32[2,648,128]{2,1,0:T(8,128)}, s32[2,648,128]{2,1,0:T(8,128)}, s32[2,648,128]{2,1,0:T(8,128)}, s32[2,648,128]{2,1,0:T(8,128)}) custom-call(s32[4]{0:T(128)} %source_ref.13, s32[4]{0:T(128)} %iota_xor_fusion.target_ref, bf16[8,32,128,128]{3,2,1,0:T(8,128)(2,1)} %orbital_ref.17, bf16[256,256]{1,0:T(8,128)(2,1)} %copy.19.wz_ref, ...), custom_call_target="tpu_custom_call" | custom-call | flops 5368709120 | bytes 1310720 | tf_op jit(solution)/shard_map/forward_zy/pallas_call | solution.py:179
  168.1 2.5 collective-permute-start.32
  171.8 36.5 %collective-permute-done.11.rest_6_ = s32[4,264,128]{2,1,0:T(8,128)S(1)} collective-permute-done((s32[4,264,128]{2,1,0:T(8,128)}, s32[4,264,128]{2,1,0:T(8,128)S(1)}, u32[]{:S(2)}, u32[]{:S(2)}) %collective-permute-start.11) | collective-permute-done | bytes 540704 | tf_op jit(solution)/shard_map/ppermute | solution.py:299
  208.2 23.3 %forward_zy.13 = (s32[2,648,128]{2,1,0:T(8,128)}, s32[2,648,128]{2,1,0:T(8,128)}, s32[2,648,128]{2,1,0:T(8,128)}, s32[2,648,128]{2,1,0:T(8,128)}) custom-call(s32[4]{0:T(128)} %source_ref.13, s32[4]{0:T(128)} %iota_xor_fusion.target_ref, bf16[8,32,128,128]{3,2,1,0:T(8,128)(2,1)} %orbital_ref.17, bf16[256,256]{1,0:T(8,128)(2,1)} %copy.19.wz_ref, ...), custom_call_target="tpu_custom_call" | custom-call | flops 5368709120 | bytes 1310720 | tf_op jit(solution)/shard_map/forward_zy/pallas_call | solution.py:179
  231.6 3.5 collective-permute-start.30
  235.1 14.1 %forward_zy.12 = (s32[1,648,128]{2,1,0:T(8,128)}, s32[1,648,128]{2,1,0:T(8,128)}, s32[1,648,128]{2,1,0:T(8,128)}, s32[1,648,128]{2,1,0:T(8,128)}) custom-call(s32[4]{0:T(128)} %source_ref.13, s32[4]{0:T(128)} %iota_xor_fusion.target_ref, bf16[8,32,128,128]{3,2,1,0:T(8,128)(2,1)} %orbital_ref.17, bf16[256,256]{1,0:T(8,128)(2,1)} %copy.19.wz_ref, ...), custom_call_target="tpu_custom_call" | custom-call | flops 2684354560 | bytes 655360 | tf_op jit(solution)/shard_map/forward_zy/pallas_call | solution.py:179
  249.2 14.1 %forward_zy.11 = (s32[1,648,128]{2,1,0:T(8,128)}, s32[1,648,128]{2,1,0:T(8,128)}, s32[1,648,128]{2,1,0:T(8,128)}, s32[1,648,128]{2,1,0:T(8,128)}) custom-call(s32[4]{0:T(128)} %source_ref.13, s32[4]{0:T(128)} %iota_xor_fusion.target_ref, bf16[8,32,128,128]{3,2,1,0:T(8,128)(2,1)} %orbital_ref.17, bf16[256,256]{1,0:T(8,128)(2,1)} %copy.19.wz_ref, ...), custom_call_target="tpu_custom_call" | custom-call | flops 2684354560 | bytes 655360 | tf_op jit(solution)/shard_map/forward_zy/pallas_call | solution.py:179
  263.9 11.8 %collective-permute-start.19 = (s32[2,648,128]{2,1,0:T(8,128)}, s32[2,648,128]{2,1,0:T(8,128)S(1)}, u32[]{:S(2)}, u32[]{:S(2)}) collective-permute-start(s32[2,648,128]{2,1,0:T(8,128)} %get-tuple-element.58), channel_id=1, source_target_pairs={{0,1},{1,0},{2,3},{3,2},{4,5},{5,4},{6,7},{7,6},{8,9},{9,8},{10,11... | collective-permute-start | bytes 1990664 | tf_op jit(solution)/shard_map/ppermute | solution.py:299
  275.7 2.5 collective-permute-start.20
  278.2 34.1 %collective-permute-done.29.rest_10_ = s32[2,648,128]{2,1,0:T(8,128)S(1)} collective-permute-done((s32[2,648,128]{2,1,0:T(8,128)}, s32[2,648,128]{2,1,0:T(8,128)S(1)}, u32[]{:S(2)}, u32[]{:S(2)}) %collective-permute-start.29) | collective-permute-done | bytes 663584 | tf_op jit(solution)/shard_map/ppermute | solution.py:299
  312.2 3.4 collective-permute-start.21
  315.6 10.7 %final_x.5.rest_12_ = f32[8,4,1024,128]{3,2,1,0:T(8,128)} custom-call(f32[16]{0:T(128)} %fusion.25.ky_ref, f32[8]{0:T(128)} %energy_ref.9, bf16[256,256]{1,0:T(8,128)(2,1)} %fusion.3.tx_ref, f32[64,128]{1,0:T(8,128)} %add_multiply_fusion.kinetic_ref, s32[4,136,128]{2,1,0:T(8,128)} %get-tuple-element.61.rest_0_, s32[4,136,128]{2,1,0:T(8,128)} %copy-done.10, ...), custom_call_target="tpu_custom_call" | custom-call | flops 4294967296 | bytes 6291456 | tf_op jit(solution)/shard_map/final_x/pallas_call | solution.py:273
  326.4 7.8 %collective-permute-start.16 = (s32[1,648,128]{2,1,0:T(8,128)S(1)}, s32[1,648,128]{2,1,0:T(8,128)S(1)}, u32[]{:S(2)}, u32[]{:S(2)}) collective-permute-start(s32[1,648,128]{2,1,0:T(8,128)S(1)} %copy-done.42), channel_id=1, source_target_pairs={{0,1},{1,0},{2,3},{3,2},{4,5},{5,4},{6,7},{7,6},{8,9},{9,8},{10,11... | collective-permute-start | bytes 995336 | tf_op jit(solution)/shard_map/ppermute | solution.py:299
  334.3 10.9 %final_x.6.rest_12_ = f32[8,4,1024,128]{3,2,1,0:T(8,128)} custom-call(f32[16]{0:T(128)} %fusion.25.ky_ref, f32[8]{0:T(128)} %energy_ref.9, bf16[256,256]{1,0:T(8,128)(2,1)} %fusion.3.tx_ref, f32[64,128]{1,0:T(8,128)} %add_multiply_fusion.kinetic_ref, s32[4,136,128]{2,1,0:T(8,128)} %get-tuple-element.61.rest_0_, ...), custom_call_target="tpu_custom_call", output_to_operand_aliasing={{}: (16, {})} | custom-call | flops 4294967296 | bytes 6291456 | tf_op jit(solution)/shard_map/final_x/pallas_call | solution.py:273
  345.2 2.7 collective-permute-start.17
  348.0 0.7 collective-permute-start.18
  349.3 24.3 %collective-permute-done.20.rest_10_ = s32[2,648,128]{2,1,0:T(8,128)S(1)} collective-permute-done((s32[2,648,128]{2,1,0:T(8,128)}, s32[2,648,128]{2,1,0:T(8,128)S(1)}, u32[]{:S(2)}, u32[]{:S(2)}) %collective-permute-start.20) | collective-permute-done | bytes 663584 | tf_op jit(solution)/shard_map/ppermute | solution.py:299
  373.7 3.4 collective-permute-start.15
  377.1 11.0 %final_x.7.rest_12_ = f32[8,4,1024,128]{3,2,1,0:T(8,128)} custom-call(f32[16]{0:T(128)} %fusion.25.ky_ref, f32[8]{0:T(128)} %energy_ref.9, bf16[256,256]{1,0:T(8,128)(2,1)} %fusion.3.tx_ref, f32[64,128]{1,0:T(8,128)} %add_multiply_fusion.kinetic_ref, s32[4,136,128]{2,1,0:T(8,128)} %get-tuple-element.41.rest_0_, ...), custom_call_target="tpu_custom_call", output_to_operand_aliasing={{}: (16, {})} | custom-call | flops 4294967296 | bytes 6291456 | tf_op jit(solution)/shard_map/final_x/pallas_call | solution.py:273
  388.1 21.1 %collective-permute-done.17.rest_10_ = s32[1,648,128]{2,1,0:T(8,128)S(1)} collective-permute-done((s32[1,648,128]{2,1,0:T(8,128)S(1)}, s32[1,648,128]{2,1,0:T(8,128)S(1)}, u32[]{:S(2)}, u32[]{:S(2)}) %collective-permute-start.17) | collective-permute-done | bytes 331808 | tf_op jit(solution)/shard_map/ppermute | solution.py:299
  409.2 0.7 copy-done.32
  410.0 7.0 %final_x.8.rest_12_ = f32[8,4,1024,128]{3,2,1,0:T(8,128)} custom-call(f32[16]{0:T(128)} %fusion.25.ky_ref, f32[8]{0:T(128)} %energy_ref.9, bf16[256,256]{1,0:T(8,128)(2,1)} %fusion.3.tx_ref, f32[64,128]{1,0:T(8,128)} %add_multiply_fusion.kinetic_ref, s32[4,136,128]{2,1,0:T(8,128)} %get-tuple-element.41.rest_0_, ...), custom_call_target="tpu_custom_call", output_to_operand_aliasing={{}: (16, {})} | custom-call | flops 2147483648 | bytes 3145728 | tf_op jit(solution)/shard_map/final_x/pallas_call | solution.py:273
  417.1 6.3 %collective-permute-done.14.rest_10_ = s32[1,648,128]{2,1,0:T(8,128)S(1)} collective-permute-done((s32[1,648,128]{2,1,0:T(8,128)S(1)}, s32[1,648,128]{2,1,0:T(8,128)S(1)}, u32[]{:S(2)}, u32[]{:S(2)}) %collective-permute-start.14) | collective-permute-done | bytes 331808 | tf_op jit(solution)/shard_map/ppermute | solution.py:299
  423.4 0.7 copy-done.31
  424.2 7.0 %final_x.9 = f32[8,4,1024,128]{3,2,1,0:T(8,128)} custom-call(f32[16]{0:T(128)} %fusion.25.ky_ref, f32[8]{0:T(128)} %energy_ref.9, bf16[256,256]{1,0:T(8,128)(2,1)} %fusion.3.tx_ref, f32[64,128]{1,0:T(8,128)} %add_multiply_fusion.kinetic_ref, s32[4,136,128]{2,1,0:T(8,128)} %get-tuple-element.41.rest_0_, ...), custom_call_target="tpu_custom_call", output_to_operand_aliasing={{}: (16, {})} | custom-call | flops 2147483648 | bytes 3145728 | tf_op jit(solution)/shard_map/final_x/pallas_call | solution.py:273
  (154 shorter events, 11.8 us)
Async XLA Ops:
  6.5 61.6 %all-gather.5.cloned.1.call-start = ((), (), s32[]{:S(2)}) async-start(), calls=%async_computation | async-start | bytes 4718592 | tf_op jit(solution)/shard_map/all_gather | solution.py:347
  8.5 111.7 %all-gather.7.cloned.1.call-start = ((), (), s32[]{:S(2)}) async-start(), calls=%async_computation.1 | async-start | bytes 11796480 | tf_op jit(solution)/shard_map/all_gather | solution.py:347
  12.1 13.3 %collective-permute-start.5 = (bf16[2,4,128,128]{3,2,1,0:T(8,128)(2,1)S(1)}, bf16[2,4,128,128]{3,2,1,0:T(8,128)(2,1)S(1)}, u32[]{:S(2)}, u32[]{:S(2)}) collective-permute-start(bf16[2,4,128,128]{3,2,1,0:T(8,128)(2,1)S(1)} %slice.27.rest_0_), channel_id=1, source_target_pairs={{0,24},{4,28},{8,16},{12,20},{16,8},{20,12},{24,0},{28,4},{1,25},{... | collective-permute-start | bytes 786440 | tf_op jit(solution)/shard_map/ppermute | solution.py:299
  16.0 17.1 %collective-permute-start.3 = (bf16[2,4,128,128]{3,2,1,0:T(8,128)(2,1)S(1)}, bf16[2,4,128,128]{3,2,1,0:T(8,128)(2,1)S(1)}, u32[]{:S(2)}, u32[]{:S(2)}) collective-permute-start(bf16[2,4,128,128]{3,2,1,0:T(8,128)(2,1)S(1)} %slice.27.rest_0_), channel_id=1, source_target_pairs={{0,16},{4,20},{8,24},{12,28},{16,0},{20,4},{24,8},{28,12},{1,17},{... | collective-permute-start | bytes 786440 | tf_op jit(solution)/shard_map/ppermute | solution.py:299
  16.5 17.3 %collective-permute-start.1 = (bf16[2,4,128,128]{3,2,1,0:T(8,128)(2,1)S(1)}, bf16[2,4,128,128]{3,2,1,0:T(8,128)(2,1)S(1)}, u32[]{:S(2)}, u32[]{:S(2)}) collective-permute-start(bf16[2,4,128,128]{3,2,1,0:T(8,128)(2,1)S(1)} %slice.27.rest_0_), channel_id=1, source_target_pairs={{0,8},{4,12},{8,0},{12,4},{16,24},{20,28},{24,16},{28,20},{1,9},{5... | collective-permute-start | bytes 786440 | tf_op jit(solution)/shard_map/ppermute | solution.py:299
  16.7 19.3 %collective-permute-start = (bf16[2,4,128,128]{3,2,1,0:T(8,128)(2,1)S(1)}, bf16[2,4,128,128]{3,2,1,0:T(8,128)(2,1)S(1)}, u32[]{:S(2)}, u32[]{:S(2)}) collective-permute-start(bf16[2,4,128,128]{3,2,1,0:T(8,128)(2,1)S(1)} %slice.27.rest_0_), channel_id=1, source_target_pairs={{0,4},{4,0},{8,12},{12,8},{16,20},{20,16},{24,28},{28,24},{1,5},{5... | collective-permute-start | bytes 786440 | tf_op jit(solution)/shard_map/ppermute | solution.py:299
  25.3 10.6 %collective-permute-start.6 = (bf16[2,4,128,128]{3,2,1,0:T(8,128)(2,1)S(1)}, bf16[2,4,128,128]{3,2,1,0:T(8,128)(2,1)S(1)}, u32[]{:S(2)}, u32[]{:S(2)}) collective-permute-start(bf16[2,4,128,128]{3,2,1,0:T(8,128)(2,1)S(1)} %collective-permute-done.5.rest_6_), channel_id=1, source_target_pairs={{0,4},{4,0},{8,12},{12,8},{16,20},{20,16},{24,28},{28,24},{1,5},{5... | collective-permute-start | bytes 786440 | tf_op jit(solution)/shard_map/ppermute | solution.py:299
  33.2 2.8 collective-permute-start.4
  33.9 2.1 collective-permute-start.2
  48.6 37.9 %collective-permute-start.22 = (s32[4,136,128]{2,1,0:T(8,128)}, s32[4,136,128]{2,1,0:T(8,128)S(1)}, u32[]{:S(2)}, u32[]{:S(2)}) collective-permute-start(s32[4,136,128]{2,1,0:T(8,128)} %get-tuple-element.62), channel_id=1, source_target_pairs={{0,1},{1,0},{2,3},{3,2},{4,5},{5,4},{6,7},{7,6},{8,9},{9,8},{10,11... | collective-permute-start | bytes 835592 | tf_op jit(solution)/shard_map/ppermute | solution.py:299
  50.1 36.8 %collective-permute-start.23 = (s32[4,136,128]{2,1,0:T(8,128)}, s32[4,136,128]{2,1,0:T(8,128)S(1)}, u32[]{:S(2)}, u32[]{:S(2)}) collective-permute-start(s32[4,136,128]{2,1,0:T(8,128)} %get-tuple-element.63), channel_id=1, source_target_pairs={{0,2},{1,3},{2,0},{3,1},{4,6},{5,7},{6,4},{7,5},{8,10},{9,11},{10,... | collective-permute-start | bytes 835592 | tf_op jit(solution)/shard_map/ppermute | solution.py:299
  52.9 53.1 %collective-permute-start.24 = (s32[4,136,128]{2,1,0:T(8,128)}, s32[4,136,128]{2,1,0:T(8,128)S(1)}, u32[]{:S(2)}, u32[]{:S(2)}) collective-permute-start(s32[4,136,128]{2,1,0:T(8,128)} %get-tuple-element.64), channel_id=1, source_target_pairs={{0,3},{1,2},{2,1},{3,0},{4,7},{5,6},{6,5},{7,4},{8,11},{9,10},{10,... | collective-permute-start | bytes 835592 | tf_op jit(solution)/shard_map/ppermute | solution.py:299
  63.9 45.6 %collective-permute-start.7 = (s32[4,136,128]{2,1,0:T(8,128)}, s32[4,136,128]{2,1,0:T(8,128)S(1)}, u32[]{:S(2)}, u32[]{:S(2)}) collective-permute-start(s32[4,136,128]{2,1,0:T(8,128)} %get-tuple-element.42), channel_id=1, source_target_pairs={{0,1},{1,0},{2,3},{3,2},{4,5},{5,4},{6,7},{7,6},{8,9},{9,8},{10,11... | collective-permute-start | bytes 835592 | tf_op jit(solution)/shard_map/ppermute | solution.py:299
  64.5 45.5 %collective-permute-start.8 = (s32[4,136,128]{2,1,0:T(8,128)}, s32[4,136,128]{2,1,0:T(8,128)S(1)}, u32[]{:S(2)}, u32[]{:S(2)}) collective-permute-start(s32[4,136,128]{2,1,0:T(8,128)} %get-tuple-element.43), channel_id=1, source_target_pairs={{0,2},{1,3},{2,0},{3,1},{4,6},{5,7},{6,4},{7,5},{8,10},{9,11},{10,... | collective-permute-start | bytes 835592 | tf_op jit(solution)/shard_map/ppermute | solution.py:299
  86.5 23.7 %collective-permute-start.9 = (s32[4,136,128]{2,1,0:T(8,128)}, s32[4,136,128]{2,1,0:T(8,128)S(1)}, u32[]{:S(2)}, u32[]{:S(2)}) collective-permute-start(s32[4,136,128]{2,1,0:T(8,128)} %get-tuple-element.44), channel_id=1, source_target_pairs={{0,3},{1,2},{2,1},{3,0},{4,7},{5,6},{6,5},{7,4},{8,11},{9,10},{10,... | collective-permute-start | bytes 835592 | tf_op jit(solution)/shard_map/ppermute | solution.py:299
  86.9 56.4 %collective-permute-start.25 = (s32[4,264,128]{2,1,0:T(8,128)}, s32[4,264,128]{2,1,0:T(8,128)S(1)}, u32[]{:S(2)}, u32[]{:S(2)}) collective-permute-start(s32[4,264,128]{2,1,0:T(8,128)} %get-tuple-element.66), channel_id=1, source_target_pairs={{0,1},{1,0},{2,3},{3,2},{4,5},{5,4},{6,7},{7,6},{8,9},{9,8},{10,11... | collective-permute-start | bytes 1622024 | tf_op jit(solution)/shard_map/ppermute | solution.py:299
  105.9 62.2 %collective-permute-start.26 = (s32[4,264,128]{2,1,0:T(8,128)}, s32[4,264,128]{2,1,0:T(8,128)S(1)}, u32[]{:S(2)}, u32[]{:S(2)}) collective-permute-start(s32[4,264,128]{2,1,0:T(8,128)} %get-tuple-element.67), channel_id=1, source_target_pairs={{0,2},{1,3},{2,0},{3,1},{4,6},{5,7},{6,4},{7,5},{8,10},{9,11},{10,... | collective-permute-start | bytes 1622024 | tf_op jit(solution)/shard_map/ppermute | solution.py:299
  109.5 58.6 %copy-start.3 = (s32[4,136,128]{2,1,0:T(8,128)}, s32[4,136,128]{2,1,0:T(8,128)S(1)}, u32[]{:S(2)}) copy-start(s32[4,136,128]{2,1,0:T(8,128)S(1)} %collective-permute-done.7.rest_1_) | copy-start | bytes 835588
  109.5 61.1 %collective-permute-start.27 = (s32[4,264,128]{2,1,0:T(8,128)}, s32[4,264,128]{2,1,0:T(8,128)S(1)}, u32[]{:S(2)}, u32[]{:S(2)}) collective-permute-start(s32[4,264,128]{2,1,0:T(8,128)} %get-tuple-element.68), channel_id=1, source_target_pairs={{0,3},{1,2},{2,1},{3,0},{4,7},{5,6},{6,5},{7,4},{8,11},{9,10},{10,... | collective-permute-start | bytes 1622024 | tf_op jit(solution)/shard_map/ppermute | solution.py:299
  110.0 58.0 %copy-start.4 = (s32[4,136,128]{2,1,0:T(8,128)}, s32[4,136,128]{2,1,0:T(8,128)S(1)}, u32[]{:S(2)}) copy-start(s32[4,136,128]{2,1,0:T(8,128)S(1)} %collective-permute-done.8.rest_2_) | copy-start | bytes 835588
  110.0 61.1 %collective-permute-start.10 = (s32[4,264,128]{2,1,0:T(8,128)}, s32[4,264,128]{2,1,0:T(8,128)S(1)}, u32[]{:S(2)}, u32[]{:S(2)}) collective-permute-start(s32[4,264,128]{2,1,0:T(8,128)} %get-tuple-element.46), channel_id=1, source_target_pairs={{0,1},{1,0},{2,3},{3,2},{4,5},{5,4},{6,7},{7,6},{8,9},{9,8},{10,11... | collective-permute-start | bytes 1622024 | tf_op jit(solution)/shard_map/ppermute | solution.py:299
  110.3 57.8 %copy-start.5 = (s32[4,136,128]{2,1,0:T(8,128)}, s32[4,136,128]{2,1,0:T(8,128)S(1)}, u32[]{:S(2)}) copy-start(s32[4,136,128]{2,1,0:T(8,128)S(1)} %collective-permute-done.9.rest_3_) | copy-start | bytes 835588
  110.3 98.0 %collective-permute-start.11 = (s32[4,264,128]{2,1,0:T(8,128)}, s32[4,264,128]{2,1,0:T(8,128)S(1)}, u32[]{:S(2)}, u32[]{:S(2)}) collective-permute-start(s32[4,264,128]{2,1,0:T(8,128)} %get-tuple-element.47), channel_id=1, source_target_pairs={{0,2},{1,3},{2,0},{3,1},{4,6},{5,7},{6,4},{7,5},{8,10},{9,11},{10,... | collective-permute-start | bytes 1622024 | tf_op jit(solution)/shard_map/ppermute | solution.py:299
  143.4 88.2 %copy-start.7 = (s32[4,264,128]{2,1,0:T(8,128)}, s32[4,264,128]{2,1,0:T(8,128)S(1)}, u32[]{:S(2)}) copy-start(s32[4,264,128]{2,1,0:T(8,128)S(1)} %collective-permute-done.25.rest_5_) | copy-start | bytes 1622020
  143.4 88.2 %collective-permute-start.31 = (s32[2,648,128]{2,1,0:T(8,128)}, s32[2,648,128]{2,1,0:T(8,128)S(1)}, u32[]{:S(2)}, u32[]{:S(2)}) collective-permute-start(s32[2,648,128]{2,1,0:T(8,128)} %get-tuple-element.74), channel_id=1, source_target_pairs={{0,1},{1,0},{2,3},{3,2},{4,5},{5,4},{6,7},{7,6},{8,9},{9,8},{10,11... | collective-permute-start | bytes 1990664 | tf_op jit(solution)/shard_map/ppermute | solution.py:299
  168.1 81.1 %copy-start.8 = (s32[4,264,128]{2,1,0:T(8,128)}, s32[4,264,128]{2,1,0:T(8,128)S(1)}, u32[]{:S(2)}) copy-start(s32[4,264,128]{2,1,0:T(8,128)S(1)} %collective-permute-done.26.rest_6_) | copy-start | bytes 1622020
  168.1 95.3 %collective-permute-start.32 = (s32[2,648,128]{2,1,0:T(8,128)S(1)}, s32[2,648,128]{2,1,0:T(8,128)S(1)}, u32[]{:S(2)}, u32[]{:S(2)}) collective-permute-start(s32[2,648,128]{2,1,0:T(8,128)S(1)} %copy-done.36), channel_id=1, source_target_pairs={{0,2},{1,3},{2,0},{3,1},{4,6},{5,7},{6,4},{7,5},{8,10},{9,11},{10,... | collective-permute-start | bytes 1990664 | tf_op jit(solution)/shard_map/ppermute | solution.py:299
  170.6 78.6 %copy-start.9 = (s32[4,264,128]{2,1,0:T(8,128)}, s32[4,264,128]{2,1,0:T(8,128)S(1)}, u32[]{:S(2)}) copy-start(s32[4,264,128]{2,1,0:T(8,128)S(1)} %collective-permute-done.27.rest_7_) | copy-start | bytes 1622020
  170.6 93.3 %collective-permute-start.33 = (s32[2,648,128]{2,1,0:T(8,128)S(1)}, s32[2,648,128]{2,1,0:T(8,128)S(1)}, u32[]{:S(2)}, u32[]{:S(2)}) collective-permute-start(s32[2,648,128]{2,1,0:T(8,128)S(1)} %copy-done.35), channel_id=1, source_target_pairs={{0,3},{1,2},{2,1},{3,0},{4,7},{5,6},{6,5},{7,4},{8,11},{9,10},{10,... | collective-permute-start | bytes 1990664 | tf_op jit(solution)/shard_map/ppermute | solution.py:299
  171.2 78.1 %copy-start = (s32[4,264,128]{2,1,0:T(8,128)}, s32[4,264,128]{2,1,0:T(8,128)S(1)}, u32[]{:S(2)}) copy-start(s32[4,264,128]{2,1,0:T(8,128)S(1)} %collective-permute-done.10.rest_5_) | copy-start | bytes 1622020
  171.2 104.5 %collective-permute-start.28 = (s32[2,648,128]{2,1,0:T(8,128)}, s32[2,648,128]{2,1,0:T(8,128)S(1)}, u32[]{:S(2)}, u32[]{:S(2)}) collective-permute-start(s32[2,648,128]{2,1,0:T(8,128)} %get-tuple-element.70), channel_id=1, source_target_pairs={{0,1},{1,0},{2,3},{3,2},{4,5},{5,4},{6,7},{7,6},{8,9},{9,8},{10,11... | collective-permute-start | bytes 1990664 | tf_op jit(solution)/shard_map/ppermute | solution.py:299
  208.2 104.0 %collective-permute-start.29 = (s32[2,648,128]{2,1,0:T(8,128)}, s32[2,648,128]{2,1,0:T(8,128)S(1)}, u32[]{:S(2)}, u32[]{:S(2)}) collective-permute-start(s32[2,648,128]{2,1,0:T(8,128)} %get-tuple-element.71), channel_id=1, source_target_pairs={{0,2},{1,3},{2,0},{3,1},{4,6},{5,7},{6,4},{7,5},{8,10},{9,11},{10,... | collective-permute-start | bytes 1990664 | tf_op jit(solution)/shard_map/ppermute | solution.py:299
  231.6 94.8 %collective-permute-start.30 = (s32[2,648,128]{2,1,0:T(8,128)}, s32[2,648,128]{2,1,0:T(8,128)S(1)}, u32[]{:S(2)}, u32[]{:S(2)}) collective-permute-start(s32[2,648,128]{2,1,0:T(8,128)} %get-tuple-element.72), channel_id=1, source_target_pairs={{0,3},{1,2},{2,1},{3,0},{4,7},{5,6},{6,5},{7,4},{8,11},{9,10},{10,... | collective-permute-start | bytes 1990664 | tf_op jit(solution)/shard_map/ppermute | solution.py:299
  263.4 63.0 %copy-start.42 = (s32[1,648,128]{2,1,0:T(8,128)S(1)}, s32[1,648,128]{2,1,0:T(8,128)}, u32[]{:S(2)}) copy-start(s32[1,648,128]{2,1,0:T(8,128)} %get-tuple-element.54) | copy-start | bytes 995332
  263.4 52.2 %copy-start.21 = (s32[2,648,128]{2,1,0:T(8,128)}, s32[2,648,128]{2,1,0:T(8,128)S(1)}, u32[]{:S(2)}) copy-start(s32[2,648,128]{2,1,0:T(8,128)S(1)} %collective-permute-done.32.rest_10_) | copy-start | bytes 1990660
  263.4 81.8 %collective-permute-start.12 = (s32[4,264,128]{2,1,0:T(8,128)}, s32[4,264,128]{2,1,0:T(8,128)S(1)}, u32[]{:S(2)}, u32[]{:S(2)}) collective-permute-start(s32[4,264,128]{2,1,0:T(8,128)} %get-tuple-element.48), channel_id=1, source_target_pairs={{0,3},{1,2},{2,1},{3,0},{4,7},{5,6},{6,5},{7,4},{8,11},{9,10},{10,... | collective-permute-start | bytes 1622024 | tf_op jit(solution)/shard_map/ppermute | solution.py:299
  263.9 51.7 %copy-start.22 = (s32[2,648,128]{2,1,0:T(8,128)}, s32[2,648,128]{2,1,0:T(8,128)S(1)}, u32[]{:S(2)}) copy-start(s32[2,648,128]{2,1,0:T(8,128)S(1)} %collective-permute-done.33.rest_11_) | copy-start | bytes 1990660
  263.9 84.8 %collective-permute-start.19 = (s32[2,648,128]{2,1,0:T(8,128)}, s32[2,648,128]{2,1,0:T(8,128)S(1)}, u32[]{:S(2)}, u32[]{:S(2)}) collective-permute-start(s32[2,648,128]{2,1,0:T(8,128)} %get-tuple-element.58), channel_id=1, source_target_pairs={{0,1},{1,0},{2,3},{3,2},{4,5},{5,4},{6,7},{7,6},{8,9},{9,8},{10,11... | collective-permute-start | bytes 1990664 | tf_op jit(solution)/shard_map/ppermute | solution.py:299
  275.7 58.5 %copy-start.23 = (s32[2,648,128]{2,1,0:T(8,128)}, s32[2,648,128]{2,1,0:T(8,128)S(1)}, u32[]{:S(2)}) copy-start(s32[2,648,128]{2,1,0:T(8,128)S(1)} %collective-permute-done.28.rest_9_) | copy-start | bytes 1990660
  275.7 97.9 %collective-permute-start.20 = (s32[2,648,128]{2,1,0:T(8,128)}, s32[2,648,128]{2,1,0:T(8,128)S(1)}, u32[]{:S(2)}, u32[]{:S(2)}) collective-permute-start(s32[2,648,128]{2,1,0:T(8,128)} %get-tuple-element.59), channel_id=1, source_target_pairs={{0,2},{1,3},{2,0},{3,1},{4,6},{5,7},{6,4},{7,5},{8,10},{9,11},{10,... | collective-permute-start | bytes 1990664 | tf_op jit(solution)/shard_map/ppermute | solution.py:299
  312.2 61.4 %collective-permute-start.21 = (s32[2,648,128]{2,1,0:T(8,128)}, s32[2,648,128]{2,1,0:T(8,128)S(1)}, u32[]{:S(2)}, u32[]{:S(2)}) collective-permute-start(s32[2,648,128]{2,1,0:T(8,128)} %get-tuple-element.60), channel_id=1, source_target_pairs={{0,3},{1,2},{2,1},{3,0},{4,7},{5,6},{6,5},{7,4},{8,11},{9,10},{10,... | collective-permute-start | bytes 1990664 | tf_op jit(solution)/shard_map/ppermute | solution.py:299
  326.4 21.6 %collective-permute-start.16 = (s32[1,648,128]{2,1,0:T(8,128)S(1)}, s32[1,648,128]{2,1,0:T(8,128)S(1)}, u32[]{:S(2)}, u32[]{:S(2)}) collective-permute-start(s32[1,648,128]{2,1,0:T(8,128)S(1)} %copy-done.42), channel_id=1, source_target_pairs={{0,1},{1,0},{2,3},{3,2},{4,5},{5,4},{6,7},{7,6},{8,9},{9,8},{10,11... | collective-permute-start | bytes 995336 | tf_op jit(solution)/shard_map/ppermute | solution.py:299
  345.2 63.9 %collective-permute-start.17 = (s32[1,648,128]{2,1,0:T(8,128)S(1)}, s32[1,648,128]{2,1,0:T(8,128)S(1)}, u32[]{:S(2)}, u32[]{:S(2)}) collective-permute-start(s32[1,648,128]{2,1,0:T(8,128)S(1)} %copy-done.41), channel_id=1, source_target_pairs={{0,2},{1,3},{2,0},{3,1},{4,6},{5,7},{6,4},{7,5},{8,10},{9,11},{10,... | collective-permute-start | bytes 995336 | tf_op jit(solution)/shard_map/ppermute | solution.py:299
  347.9 61.2 %copy-start.29 = (s32[1,648,128]{2,1,0:T(8,128)}, s32[1,648,128]{2,1,0:T(8,128)S(1)}, u32[]{:S(2)}) copy-start(s32[1,648,128]{2,1,0:T(8,128)S(1)} %collective-permute-done.16.rest_9_) | copy-start | bytes 995332
  348.0 61.2 %collective-permute-start.18 = (s32[1,648,128]{2,1,0:T(8,128)S(1)}, s32[1,648,128]{2,1,0:T(8,128)S(1)}, u32[]{:S(2)}, u32[]{:S(2)}) collective-permute-start(s32[1,648,128]{2,1,0:T(8,128)S(1)} %copy-done.40), channel_id=1, source_target_pairs={{0,3},{1,2},{2,1},{3,0},{4,7},{5,6},{6,5},{7,4},{8,11},{9,10},{10,... | collective-permute-start | bytes 995336 | tf_op jit(solution)/shard_map/ppermute | solution.py:299
  348.7 68.4 %collective-permute-start.13 = (s32[1,648,128]{2,1,0:T(8,128)S(1)}, s32[1,648,128]{2,1,0:T(8,128)S(1)}, u32[]{:S(2)}, u32[]{:S(2)}) collective-permute-start(s32[1,648,128]{2,1,0:T(8,128)S(1)} %copy-done.39), channel_id=1, source_target_pairs={{0,1},{1,0},{2,3},{3,2},{4,5},{5,4},{6,7},{7,6},{8,9},{9,8},{10,11... | collective-permute-start | bytes 995336 | tf_op jit(solution)/shard_map/ppermute | solution.py:299
  373.6 49.8 %collective-permute-start.14 = (s32[1,648,128]{2,1,0:T(8,128)S(1)}, s32[1,648,128]{2,1,0:T(8,128)S(1)}, u32[]{:S(2)}, u32[]{:S(2)}) collective-permute-start(s32[1,648,128]{2,1,0:T(8,128)S(1)} %copy-done.38), channel_id=1, source_target_pairs={{0,2},{1,3},{2,0},{3,1},{4,6},{5,7},{6,4},{7,5},{8,10},{9,11},{10,... | collective-permute-start | bytes 995336 | tf_op jit(solution)/shard_map/ppermute | solution.py:299
  373.7 49.7 %collective-permute-start.15 = (s32[1,648,128]{2,1,0:T(8,128)S(1)}, s32[1,648,128]{2,1,0:T(8,128)S(1)}, u32[]{:S(2)}, u32[]{:S(2)}) collective-permute-start(s32[1,648,128]{2,1,0:T(8,128)S(1)} %copy-done.37), channel_id=1, source_target_pairs={{0,3},{1,2},{2,1},{3,0},{4,7},{5,6},{6,5},{7,4},{8,11},{9,10},{10,... | collective-permute-start | bytes 995336 | tf_op jit(solution)/shard_map/ppermute | solution.py:299
  (31 other events, 442.8 us)
Sparse Core Ops, SparseCore 0:
  9.2 45.6 all-gather.4
  56.8 63.3 all-gather.6

commit v2 on v1

--- a/solution.py
+++ b/solution.py
@@ -69,6 +69,18 @@
         turned = pltpu.roll(part[keep:], keep, 1)
         results.append(part[:keep] + jnp.where(lane < keep, -turned, turned))
     return results
+
+
+def pack_words(low, high):
+    return (high << 16) | (low & 0xFFFF)
+
+
+def unpack_words(words):
+    return [((words << 16) >> 16).astype(f32), (words >> 16).astype(f32)]
+
+
+def scale_rows(bands, patterns):
+    return pl.cdiv(bands * (patterns // 2), 8) * 8
 
 
 def forward_kernel(
@@ -134,11 +146,13 @@
     @pl.when(step == pl.num_programs(1) - 1)
     def _():
         rows = planes_total * columns
+        pairs = patterns // 2
+        start = pl.multiple_of(band * (pairs * rows), 8)
         for shift in range(parts):
             target = target_ref[shift]
-            out_ref = out_refs[shift]
-            for pair in range(patterns // 2):
-                inverse = []
+            out_ref = out_refs[shift].at[pl.ds(start, pairs * rows), :]
+            for pair in range(pairs):
+                inverse, codes = [], []
                 for pattern in (2 * pair, 2 * pair + 1):
                     top = jnp.zeros((columns, 2 * keep), f32)
                     for at in range(planes_total):
@@ -148,8 +162,9 @@
                         jnp.log(jnp.maximum(top, 1e-30) * (1.0 / code_top)) * code_steps
                     )
                     inverse.append(jnp.exp(code * (-1.0 / code_steps)))
-                    row = (patterns // 2) * rows + pattern
-                    out_ref[0, row : row + 1, :] = code.astype(jnp.int32)
+                    codes.append(code.astype(jnp.int32))
+                scale_row = pl.num_programs(0) * (pairs * rows) + band * pairs + pair
+                out_refs[shift][pl.ds(scale_row, 1), :] = pack_words(*codes)
                 for at in range(planes_total):
                     low, high = [
                         jnp.round(held[2 * pair + which, at, target] * inverse[which]).astype(
@@ -158,7 +173,7 @@
                         for which in range(2)
                     ]
                     row = pair * rows + at * columns
-                    out_ref[0, row : row + columns, :] = (high << 16) | (low & 0xFFFF)
+                    out_ref[row : row + columns, :] = pack_words(low, high)
 
 
 def forward(
@@ -169,7 +184,7 @@
     columns = keep // parts
     length = orbitals.shape[2]
     slots = len(potentials)
-    rows = (patterns // 2) * planes * columns + 8
+    rows = bands * (patterns // 2) * planes * columns + scale_rows(bands, patterns)
     kernel = functools.partial(
         forward_kernel, slots, planes, step_planes, keep, columns, patterns, parts
     )
@@ -190,14 +205,14 @@
                 fixed(ty),
             ]
             + [whole] * slots,
-            out_specs=[pl.BlockSpec((1, rows, 2 * keep), lambda b, g, *_: (b, 0, 0))] * parts,
+            out_specs=[pl.BlockSpec((rows, 2 * keep), lambda b, g, *_: (0, 0))] * parts,
             scratch_shapes=[
                 pltpu.VMEM((patterns, 2, planes, length, length), bf16),
                 pltpu.VMEM((patterns, planes, parts, columns, 2 * keep), f32),
                 pltpu.SemaphoreType.DMA((patterns,)),
             ],
         ),
-        out_shape=[jax.ShapeDtypeStruct((bands, rows, 2 * keep), jnp.int32)] * parts,
+        out_shape=[jax.ShapeDtypeStruct((rows, 2 * keep), jnp.int32)] * parts,
         compiler_params=pltpu.CompilerParams(
             dimension_semantics=("arbitrary", "arbitrary"), vmem_limit_bytes=vmem_limit
         ),
@@ -209,12 +224,12 @@
 
 
 def final_kernel(
-    plane_counts, first_band, keep, columns, patterns, parts, chained,
+    plane_counts, band_offsets, first_band, keep, columns, patterns, parts, chained,
     ky_ref, energy_ref, tx_ref, kinetic_ref, *rest
 ):
     count = len(plane_counts) * parts
-    chunk_refs = rest[:count]
-    out_ref, wide = rest[count + chained :]
+    chunk_refs, scale_refs = rest[:count], rest[count : 2 * count]
+    out_ref, wide = rest[2 * count + chained :]
     energy = energy_ref[pl.program_id(0) + first_band]
     total = parts * sum(plane_counts)
     for pair in range(patterns // 2):
@@ -222,14 +237,13 @@
         for chunk, planes in enumerate(plane_counts):
             rows = planes * columns
             for shift in range(parts):
-                ref = chunk_refs[chunk * parts + shift]
-                scales = []
-                for pattern in (2 * pair, 2 * pair + 1):
-                    row = (patterns // 2) * rows + pattern
-                    scales.append(jnp.exp(ref[0, row : row + 1, :].astype(f32) * (1.0 / code_steps)))
-                words = ref[0, pair * rows : (pair + 1) * rows, :]
-                wide[0, base : base + rows, :] = ((words << 16) >> 16).astype(f32) * scales[0]
-                wide[1, base : base + rows, :] = (words >> 16).astype(f32) * scales[1]
+                place = chunk * parts + shift
+                scale_row = (pl.program_id(0) + band_offsets[chunk]) * (patterns // 2) + pair
+                codes = unpack_words(scale_refs[place][pl.ds(scale_row, 1), :])
+                values = unpack_words(chunk_refs[place][pair * rows : (pair + 1) * rows, :])
+                for which in range(2):
+                    scale = jnp.exp(codes[which] * (1.0 / code_steps))
+                    wide[which, base : base + rows, :] = values[which] * scale
                 base += rows
 
         def two_columns(index, carry):
@@ -250,24 +264,32 @@
         lax.fori_loop(0, columns // 2, two_columns, 0, unroll=math.gcd(columns // 2, 4))
 
 
-def final(chunks, plane_counts, band_offsets, first_band, bands, held_out, ky, energy, tx, kinetic, patterns, keep, all_bands):
+def final(
+    chunks, plane_counts, band_offsets, group_bands, first_band, bands, held_out, ky, energy, tx,
+    kinetic, patterns, keep, all_bands
+):
     parts = len(chunks[0])
     columns = keep // parts
     total = parts * sum(plane_counts)
     chained = 0 if held_out is None else 1
     kernel = functools.partial(
-        final_kernel, plane_counts, first_band, keep, columns, patterns, parts, chained
+        final_kernel, plane_counts, band_offsets, first_band, keep, columns, patterns, parts, chained
     )
     fixed = lambda array: pl.BlockSpec(array.shape, lambda b, *_: (0,) * array.ndim)
-    chunk_specs = []
-    for arrays, offset in zip(chunks, band_offsets):
-        for array in arrays:
-            chunk_specs.append(
-                pl.BlockSpec((1,) + array.shape[1:], lambda b, *_, o=offset: (b + o, 0, 0))
-            )
+    chunk_specs, scale_specs = [], []
+    for arrays, offset, planes, held_bands in zip(chunks, band_offsets, plane_counts, group_bands):
+        rows = (patterns // 2) * planes * columns
+        scales = scale_rows(held_bands, patterns)
+        place = held_bands * rows // scales
+        chunk_specs += [
+            pl.BlockSpec((rows, 2 * keep), lambda b, *_, o=offset: (b + o, 0))
+        ] * parts
+        scale_specs += [
+            pl.BlockSpec((scales, 2 * keep), lambda b, *_, at=place: (at, 0))
+        ] * parts
     flat = [array for arrays in chunks for array in arrays]
     out_block = (1, patterns, keep * columns, 2 * keep)
-    operands = [ky, energy, tx, kinetic] + flat
+    operands = [ky, energy, tx, kinetic] + flat + flat
     if chained:
         operands.append(held_out)
     return pl.pallas_call(
@@ -277,6 +299,7 @@
             grid=(bands,),
             in_specs=[fixed(tx), fixed(kinetic)]
             + chunk_specs
+            + scale_specs
             + [pl.BlockSpec(memory_space=pl.ANY)] * chained,
             out_specs=pl.BlockSpec(out_block, lambda b, *_: (b + first_band, 0, 0, 0)),
             scratch_shapes=[pltpu.VMEM((2, total * columns, 2 * keep), f32)],
@@ -297,6 +320,10 @@
 
 def permute(array, axis, step):
     return lax.ppermute(array, axis, [(i, i ^ step) for i in range(lax.axis_size(axis))])
+
+
+def after(arrays, earlier):
+    return lax.optimization_barrier((arrays, earlier))[0]
 
 
 def gather_chips(block):
@@ -337,45 +364,54 @@
     chunks = [
         (start, end - start, math.gcd(start, end - start)) for start, end in zip([0] + ends, ends)
     ]
+    groups = [halves(bands), halves(bands), cut(bands)]
     band_rank = lax.axis_index("band")
-    sources = rank ^ jnp.arange(parts, dtype=jnp.int32)
+    steps = [0] + list(range(parts - 1, 0, -1))
+    sources = rank ^ jnp.array(steps, dtype=jnp.int32)
+    flipped = band_rank ^ pattern_owner
     blocks = [
         lax.slice_in_dim(potential_slots[0], start, start + planes, axis=1)
         for start, planes, _ in chunks
     ]
-    potentials = [(gather_cores(gather_chips(blocks[0])), band_rank ^ pattern_owner)]
-    potentials += [([lax.all_gather(block, "band")], pattern_owner) for block in blocks[1:]]
-
     position = jnp.arange(length, dtype=jnp.int32)
     wz = right_table(retained[2], position, length)
     ty = left_table(retained[1], position, length)
+
+    chips = gather_chips(blocks[0])
+    ready = after(chips, (wz, ty, flipped, sources))
+    slots = [(gather_cores(ready), flipped)]
+    slots += [
+        ([lax.all_gather(after(block, (chips, wz, ty)), "band")], pattern_owner) for block in blocks[1:]
+    ]
+
+    def run(chunk, first, count):
+        start, planes, step_planes = chunks[chunk]
+        return forward(
+            orbitals, *slots[chunk], sources, wz, ty, start, planes, step_planes,
+            first, count, keep, patterns
+        )
+
+    def spread(blocks):
+        return [blocks[0]] + [permute(*each) for each in zip(blocks[1:], ["plane"] * parts, steps[1:])]
+
+    made = [[run(chunk, *group) for group in groups[chunk]] for chunk in range(len(chunks))]
+    received = [[spread(blocks) for blocks in chunk_made] for chunk_made in made]
+
+    late = after(retained, made[0])
     plane_order = jnp.concatenate(
         [
             (sources[:, None] * local_planes + start + jnp.arange(planes, dtype=jnp.int32)).reshape(-1)
             for start, planes, _ in chunks
         ]
     )
-    tx = left_table(retained[0], plane_order, length)
-    ky_local = lax.dynamic_slice_in_dim(retained[1], rank * columns, columns)
-    kz = signed_square(retained[2], length)
+    tx = left_table(late[0], plane_order, length)
+    ky_local = lax.dynamic_slice_in_dim(late[1], rank * columns, columns)
+    kz = signed_square(late[2], length)
     kinetic = kinetic_coef * (
-        signed_square(retained[0], length)[:, None] + jnp.concatenate([kz, kz])[None, :]
+        signed_square(late[0], length)[:, None] + jnp.concatenate([kz, kz])[None, :]
     )
     ky = kinetic_coef * signed_square(ky_local, length)
 
-    def run(chunk, first, count):
-        start, planes, step_planes = chunks[chunk]
-        slots, source = potentials[chunk]
-        made = forward(
-            orbitals, slots, source, sources, wz, ty, start, planes, step_planes,
-            first, count, keep, patterns
-        )
-        return [made[0]] + [permute(made[s], "plane", s) for s in range(1, parts)]
-
-    groups = [halves(bands)] * (len(chunks) - 1) + [cut(bands)]
-    received = [
-        [run(chunk, first, count) for first, count in groups[chunk]] for chunk in range(len(chunks))
-    ]
     out = None
     for first, count in groups[-1]:
         places = [holder(chunk_groups, first) for chunk_groups in groups]
@@ -383,6 +419,7 @@
             [received[chunk][index] for chunk, (index, _) in enumerate(places)],
             [planes for _, planes, _ in chunks],
             [offset for _, offset in places],
+            [groups[chunk][index][1] for chunk, (index, _) in enumerate(places)],
             first, count, out, ky, band_energy, tx, kinetic, patterns, keep, bands,
         )
     return out.reshape(bands, patterns, keep, columns, 2 * keep)

time: 443 us -> 427 us (0.964)
  waiting for transfers between devices: 140 us -> 116 us
  starting transfers between devices: 64.3 us -> 74.6 us
    ppermute x34, waiting for transfers between devices: 133 us -> 103 us  [permute(): lax.ppermute(array, axis, [(i, i ^ step) for i in range(lax.axis_size(axi...]
    ppermute x34, starting transfers between devices: 64.2 us -> 74.6 us  [permute(): lax.ppermute(array, axis, [(i, i ^ step) for i in range(lax.axis_size(axi...]
    all_gather x2, waiting for transfers between devices: 6.11 us -> 13.6 us  [per_device(): lax.all_gather(after(block, (chips, wz, ty)), 'band')]
  transfers between devices with their start and end apart: 36 -> 36, of which waited for: 9 -> 14; matrix products, arithmetic and copies ran while one was open for 3% -> 3% of each run, Pallas kernels for 45% -> 46%
where the time goes in v2:
time: 427 us; the launch traced here: 426 us
  Pallas kernels  205 us (48%)
  waiting for transfers between devices  116 us (27%)
  starting transfers between devices  74.6 us (17%)
  between operations  14 us (3%)
  local copies, waits for them, and re-layouts  10.7 us (3%)
  other arithmetic  6.06 us (1%)
    pallas_call x9, Pallas kernels, forward(): pl.pallas_call(kernel, grid_spec=pltpu.PrefetchScalarGridSpec(num_scalar_...  158 us
    ppermute x34, waiting for transfers between devices, permute(): lax.ppermute(array, axis, [(i, i ^ step) for i in range(lax.axis_size(axi...  103 us
    ppermute x34, starting transfers between devices, permute(): lax.ppermute(array, axis, [(i, i ^ step) for i in range(lax.axis_size(axi...  74.6 us
    pallas_call x5, Pallas kernels, final(): pl.pallas_call(kernel, grid_spec=pltpu.PrefetchScalarGridSpec(num_scalar_...  46.5 us
    all_gather x2, waiting for transfers between devices, per_device(): lax.all_gather(after(block, (chips, wz, ty)), 'band')  13.6 us
  transfers between devices with their start and end apart: 36, of which 14 were waited for; matrix products, arithmetic and copies ran while one was open for 3% of the time, Pallas kernels for 46%

profile of v2, /device:TPU:0, one launch (start us, length us, event | category | flops | bytes accessed | tf_op | source)
XLA Modules:
  0.0 426.2 jit_solution(3429448952473121927)
XLA Ops:
  6.5 1.0 slice.33.rest_0_
  7.5 4.0 collective-permute-start.2
  12.1 0.8 slice_bitcast_fusion.1
  13.9 1.9 slice.34
  15.9 2.8 collective-permute-done.2.rest_6_
  18.7 4.7 %collective-permute-done.1.rest_4_ = bf16[2,4,128,128]{3,2,1,0:T(8,128)(2,1)S(1)} collective-permute-done((bf16[2,4,128,128]{3,2,1,0:T(8,128)(2,1)S(1)}, bf16[2,4,128,128]{3,2,1,0:T(8,128)(2,1)S(1)}, u32[]{:S(2)}, u32[]{:S(2)}) %collective-permute-start.1) | collective-permute-done | bytes 262176 | tf_op jit(solution)/shard_map/ppermute | solution.py:322
  23.8 2.6 slice.35
  26.4 0.8 copy.20.wz_ref
  27.1 1.2 broadcast_multiply_fusion
  28.6 1.2 broadcast_xor_fusion.1.source_ref
  33.6 11.0 %forward_zy.9 = (s32[520,128]{1,0:T(8,128)}, s32[520,128]{1,0:T(8,128)}, s32[520,128]{1,0:T(8,128)}, s32[520,128]{1,0:T(8,128)}) custom-call(s32[4]{0:T(128)} %broadcast_xor_fusion.1.source_ref, s32[4]{0:T(128)} %get-tuple-element.108.target_ref, bf16[8,32,128,128]{3,2,1,0:T(8,128)(2,1)} %orbital_ref.17, bf16[256,256]{1,0:T(8,128)(2,1)} %copy.20.wz_ref, ...), custom_call_target="tpu_custom_call" | custom-call | flops 2147483648 | bytes 524288 | tf_op jit(solution)/shard_map/forward_zy/pallas_call | solution.py:194
  44.6 3.7 collective-permute-start.22
  48.2 0.8 collective-permute-start.24
  49.0 11.1 %forward_zy.10 = (s32[520,128]{1,0:T(8,128)}, s32[520,128]{1,0:T(8,128)}, s32[520,128]{1,0:T(8,128)}, s32[520,128]{1,0:T(8,128)}) custom-call(s32[4]{0:T(128)} %broadcast_xor_fusion.1.source_ref, s32[4]{0:T(128)} %get-tuple-element.108.target_ref, bf16[8,32,128,128]{3,2,1,0:T(8,128)(2,1)} %orbital_ref.17, bf16[256,256]{1,0:T(8,128)(2,1)} %copy.20.wz_ref, ...), custom_call_target="tpu_custom_call" | custom-call | flops 2147483648 | bytes 524288 | tf_op jit(solution)/shard_map/forward_zy/pallas_call | solution.py:194
  60.1 3.7 collective-permute-start.7
  66.1 18.7 %forward_zy.15 = (s32[1032,128]{1,0:T(8,128)}, s32[1032,128]{1,0:T(8,128)}, s32[1032,128]{1,0:T(8,128)}, s32[1032,128]{1,0:T(8,128)}) custom-call(s32[4]{0:T(128)} %source_ref.13, s32[4]{0:T(128)} %get-tuple-element.108.target_ref, bf16[8,32,128,128]{3,2,1,0:T(8,128)(2,1)} %orbital_ref.17, bf16[256,256]{1,0:T(8,128)(2,1)} %copy.20.wz_ref, ...), custom_call_target="tpu_custom_call" | custom-call | flops 4294967296 | bytes 1048576 | tf_op jit(solution)/shard_map/forward_zy/pallas_call | solution.py:194
  84.8 0.8 collective-permute-start.9
  85.7 3.7 collective-permute-start.25
  89.4 18.7 %forward_zy.11 = (s32[1032,128]{1,0:T(8,128)}, s32[1032,128]{1,0:T(8,128)}, s32[1032,128]{1,0:T(8,128)}, s32[1032,128]{1,0:T(8,128)}) custom-call(s32[4]{0:T(128)} %source_ref.13, s32[4]{0:T(128)} %get-tuple-element.108.target_ref, bf16[8,32,128,128]{3,2,1,0:T(8,128)(2,1)} %orbital_ref.17, bf16[256,256]{1,0:T(8,128)(2,1)} %copy.20.wz_ref, ...), custom_call_target="tpu_custom_call" | custom-call | flops 4294967296 | bytes 1048576 | tf_op jit(solution)/shard_map/forward_zy/pallas_call | solution.py:194
  108.9 3.7 collective-permute-start.10
  112.7 13.6 %all-gather.7.cloned.1.call-done = bf16[16,20,128,128]{3,2,1,0:T(8,128)(2,1)} async-done(((bf16[2,20,128,128]{3,2,1,0:T(8,128)(2,1)}), bf16[16,20,128,128]{3,2,1,0:T(8,128)(2,1)}) %all-gather.7.cloned.1.call-update) | async-done | bytes 10485776 | tf_op jit(solution)/shard_map/all_gather | solution.py:384
  126.4 23.4 %forward_zy.17 = (s32[1288,128]{1,0:T(8,128)}, s32[1288,128]{1,0:T(8,128)}, s32[1288,128]{1,0:T(8,128)}, s32[1288,128]{1,0:T(8,128)}) custom-call(s32[4]{0:T(128)} %source_ref.13, s32[4]{0:T(128)} %get-tuple-element.108.target_ref, bf16[8,32,128,128]{3,2,1,0:T(8,128)(2,1)} %orbital_ref.17, bf16[256,256]{1,0:T(8,128)(2,1)} %copy.20.wz_ref, ...), custom_call_target="tpu_custom_call" | custom-call | flops 5368709120 | bytes 1310720 | tf_op jit(solution)/shard_map/forward_zy/pallas_call | solution.py:194
  149.8 3.4 collective-permute-start.31
  153.2 23.3 %forward_zy.16 = (s32[1288,128]{1,0:T(8,128)}, s32[1288,128]{1,0:T(8,128)}, s32[1288,128]{1,0:T(8,128)}, s32[1288,128]{1,0:T(8,128)}) custom-call(s32[4]{0:T(128)} %source_ref.13, s32[4]{0:T(128)} %get-tuple-element.108.target_ref, bf16[8,32,128,128]{3,2,1,0:T(8,128)(2,1)} %orbital_ref.17, bf16[256,256]{1,0:T(8,128)(2,1)} %copy.20.wz_ref, ...), custom_call_target="tpu_custom_call" | custom-call | flops 5368709120 | bytes 1310720 | tf_op jit(solution)/shard_map/forward_zy/pallas_call | solution.py:194
  177.2 3.1 collective-permute-start.33
  180.3 1.4 collective-permute-start.28
  181.6 46.4 %collective-permute-done.11.rest_6_.rest_18_ = s32[1032,128]{1,0:T(8,128)S(1)} collective-permute-done((s32[1032,128]{1,0:T(8,128)}, s32[1032,128]{1,0:T(8,128)S(1)}, u32[]{:S(2)}, u32[]{:S(2)}) %collective-permute-start.11) | collective-permute-done | bytes 528416 | tf_op jit(solution)/shard_map/ppermute | solution.py:322
  228.1 23.5 %forward_zy.14 = (s32[1288,128]{1,0:T(8,128)}, s32[1288,128]{1,0:T(8,128)}, s32[1288,128]{1,0:T(8,128)}, s32[1288,128]{1,0:T(8,128)}) custom-call(s32[4]{0:T(128)} %source_ref.13, s32[4]{0:T(128)} %get-tuple-element.108.target_ref, bf16[8,32,128,128]{3,2,1,0:T(8,128)(2,1)} %orbital_ref.17, bf16[256,256]{1,0:T(8,128)(2,1)} %copy.20.wz_ref, ...), custom_call_target="tpu_custom_call" | custom-call | flops 5368709120 | bytes 1310720 | tf_op jit(solution)/shard_map/forward_zy/pallas_call | solution.py:194
  251.6 5.3 %collective-permute-start.30 = (s32[1288,128]{1,0:T(8,128)}, s32[1288,128]{1,0:T(8,128)S(1)}, u32[]{:S(2)}, u32[]{:S(2)}) collective-permute-start(s32[1288,128]{1,0:T(8,128)} %get-tuple-element.86), channel_id=1, source_target_pairs={{0,1},{1,0},{2,3},{3,2},{4,5},{5,4},{6,7},{7,6},{8,9},{9,8},{10,11... | collective-permute-start | bytes 1978376 | tf_op jit(solution)/shard_map/ppermute | solution.py:322
  256.9 14.1 %forward_zy.13 = (s32[648,128]{1,0:T(8,128)}, s32[648,128]{1,0:T(8,128)}, s32[648,128]{1,0:T(8,128)}, s32[648,128]{1,0:T(8,128)}) custom-call(s32[4]{0:T(128)} %source_ref.13, s32[4]{0:T(128)} %get-tuple-element.108.target_ref, bf16[8,32,128,128]{3,2,1,0:T(8,128)(2,1)} %orbital_ref.17, bf16[256,256]{1,0:T(8,128)(2,1)} %copy.20.wz_ref, ...), custom_call_target="tpu_custom_call" | custom-call | flops 2684354560 | bytes 655360 | tf_op jit(solution)/shard_map/forward_zy/pallas_call | solution.py:194
  271.1 14.1 %forward_zy.12 = (s32[648,128]{1,0:T(8,128)}, s32[648,128]{1,0:T(8,128)}, s32[648,128]{1,0:T(8,128)}, s32[648,128]{1,0:T(8,128)}) custom-call(s32[4]{0:T(128)} %source_ref.13, s32[4]{0:T(128)} %get-tuple-element.108.target_ref, bf16[8,32,128,128]{3,2,1,0:T(8,128)(2,1)} %orbital_ref.17, bf16[256,256]{1,0:T(8,128)(2,1)} %copy.20.wz_ref, ...), custom_call_target="tpu_custom_call" | custom-call | flops 2684354560 | bytes 655360 | tf_op jit(solution)/shard_map/forward_zy/pallas_call | solution.py:194
  285.4 0.8 copy-done.20
  286.2 2.5 collective-permute-start.19
  288.7 1.0 collective-permute-start.20
  289.7 35.2 %collective-permute-done.29.rest_10_.rest_22_ = s32[1288,128]{1,0:T(8,128)S(1)} collective-permute-done((s32[1288,128]{1,0:T(8,128)}, s32[1288,128]{1,0:T(8,128)S(1)}, u32[]{:S(2)}, u32[]{:S(2)}) %collective-permute-start.29) | collective-permute-done | bytes 659488 | tf_op jit(solution)/shard_map/ppermute | solution.py:322
  325.3 10.6 %final_x.5.rest_24_ = f32[8,4,1024,128]{3,2,1,0:T(8,128)} custom-call(f32[16]{0:T(128)} %fusion.25.ky_ref, f32[8]{0:T(128)} %energy_ref.9, bf16[256,256]{1,0:T(8,128)(2,1)} %fusion.4.tx_ref, f32[64,128]{1,0:T(8,128)} %add_multiply_fusion.kinetic_ref, s32[520,128]{1,0:T(8,128)} %get-tuple-element.52.rest_0_.rest_12_, s32[520,128]{1,0:T(8,128)} %copy-done.9, ...), custom_call_target="tpu_custom_call" | custom-call | flops 4294967296 | bytes 6291456 | tf_op jit(solution)/shard_map/final_x/pallas_call | solution.py:295
  335.9 3.3 collective-permute-start.16
  339.3 10.8 %final_x.6.rest_24_ = f32[8,4,1024,128]{3,2,1,0:T(8,128)} custom-call(f32[16]{0:T(128)} %fusion.25.ky_ref, f32[8]{0:T(128)} %energy_ref.9, bf16[256,256]{1,0:T(8,128)(2,1)} %fusion.4.tx_ref, f32[64,128]{1,0:T(8,128)} %add_multiply_fusion.kinetic_ref, s32[520,128]{1,0:T(8,128)} %get-tuple-element.52.rest_0_.rest_12_, ...), custom_call_target="tpu_custom_call", output_to_operand_aliasing={{}: (28, {})} | custom-call | flops 4294967296 | bytes 6291456 | tf_op jit(solution)/shard_map/final_x/pallas_call | solution.py:295
  350.2 1.3 collective-permute-start.17
  351.6 25.6 %collective-permute-start.18 = (s32[648,128]{1,0:T(8,128)S(1)}, s32[648,128]{1,0:T(8,128)S(1)}, u32[]{:S(2)}, u32[]{:S(2)}) collective-permute-start(s32[648,128]{1,0:T(8,128)S(1)} %copy-done.41), channel_id=1, source_target_pairs={{0,1},{1,0},{2,3},{3,2},{4,5},{5,4},{6,7},{7,6},{8,9},{9,8},{10,11... | collective-permute-start | bytes 995336 | tf_op jit(solution)/shard_map/ppermute | solution.py:322
  377.3 2.5 collective-permute-start.13
  379.9 2.0 collective-permute-start.15
  381.9 10.9 %final_x.7.rest_24_ = f32[8,4,1024,128]{3,2,1,0:T(8,128)} custom-call(f32[16]{0:T(128)} %fusion.25.ky_ref, f32[8]{0:T(128)} %energy_ref.9, bf16[256,256]{1,0:T(8,128)(2,1)} %fusion.4.tx_ref, f32[64,128]{1,0:T(8,128)} %add_multiply_fusion.kinetic_ref, s32[520,128]{1,0:T(8,128)} %get-tuple-element.56.rest_0_.rest_12_, ...), custom_call_target="tpu_custom_call", output_to_operand_aliasing={{}: (28, {})} | custom-call | flops 4294967296 | bytes 6291456 | tf_op jit(solution)/shard_map/final_x/pallas_call | solution.py:295
  392.8 4.5 %collective-permute-done.18.rest_11_.rest_23_ = s32[648,128]{1,0:T(8,128)S(1)} collective-permute-done((s32[648,128]{1,0:T(8,128)S(1)}, s32[648,128]{1,0:T(8,128)S(1)}, u32[]{:S(2)}, u32[]{:S(2)}) %collective-permute-start.18) | collective-permute-done | bytes 331808 | tf_op jit(solution)/shard_map/ppermute | solution.py:322
  398.0 7.1 %final_x.8.rest_24_ = f32[8,4,1024,128]{3,2,1,0:T(8,128)} custom-call(f32[16]{0:T(128)} %fusion.25.ky_ref, f32[8]{0:T(128)} %energy_ref.9, bf16[256,256]{1,0:T(8,128)(2,1)} %fusion.4.tx_ref, f32[64,128]{1,0:T(8,128)} %add_multiply_fusion.kinetic_ref, s32[520,128]{1,0:T(8,128)} %get-tuple-element.56.rest_0_.rest_12_, ...), custom_call_target="tpu_custom_call", output_to_operand_aliasing={{}: (28, {})} | custom-call | flops 2147483648 | bytes 3145728 | tf_op jit(solution)/shard_map/final_x/pallas_call | solution.py:295
  405.1 6.4 %collective-permute-done.14.rest_10_.rest_22_ = s32[648,128]{1,0:T(8,128)S(1)} collective-permute-done((s32[648,128]{1,0:T(8,128)S(1)}, s32[648,128]{1,0:T(8,128)S(1)}, u32[]{:S(2)}, u32[]{:S(2)}) %collective-permute-start.14) | collective-permute-done | bytes 331808 | tf_op jit(solution)/shard_map/ppermute | solution.py:322
  411.5 0.7 copy-done.24
  412.3 7.1 %final_x.9 = f32[8,4,1024,128]{3,2,1,0:T(8,128)} custom-call(f32[16]{0:T(128)} %fusion.25.ky_ref, f32[8]{0:T(128)} %energy_ref.9, bf16[256,256]{1,0:T(8,128)(2,1)} %fusion.4.tx_ref, f32[64,128]{1,0:T(8,128)} %add_multiply_fusion.kinetic_ref, s32[520,128]{1,0:T(8,128)} %get-tuple-element.56.rest_0_.rest_12_, ...), custom_call_target="tpu_custom_call", output_to_operand_aliasing={{}: (28, {})} | custom-call | flops 2147483648 | bytes 3145728 | tf_op jit(solution)/shard_map/final_x/pallas_call | solution.py:295
  (155 shorter events, 11.4 us)
Async XLA Ops:
  6.5 57.2 %copy-start.35 = (s32[3,64]{1,0:T(4,128)S(1)}, s32[3,64]{1,0:T(4,128)}, u32[]{:S(2)}) copy-start(s32[3,64]{1,0:T(4,128)} %param.9) | copy-start | bytes 2308
  6.5 59.6 %all-gather.5.cloned.1.call-start = ((), (), s32[]{:S(2)}) async-start(), calls=%async_computation | async-start | bytes 4718592 | tf_op jit(solution)/shard_map/all_gather | solution.py:384
  7.5 11.1 %collective-permute-start.2 = (bf16[2,4,128,128]{3,2,1,0:T(8,128)(2,1)S(1)}, bf16[2,4,128,128]{3,2,1,0:T(8,128)(2,1)S(1)}, u32[]{:S(2)}, u32[]{:S(2)}) collective-permute-start(bf16[2,4,128,128]{3,2,1,0:T(8,128)(2,1)S(1)} %slice.33.rest_0_), channel_id=1, source_target_pairs={{0,24},{4,28},{8,16},{12,20},{16,8},{20,12},{24,0},{28,4},{1,25},{... | collective-permute-start | bytes 786440 | tf_op jit(solution)/shard_map/ppermute | solution.py:322
  11.5 11.9 %collective-permute-start.1 = (bf16[2,4,128,128]{3,2,1,0:T(8,128)(2,1)S(1)}, bf16[2,4,128,128]{3,2,1,0:T(8,128)(2,1)S(1)}, u32[]{:S(2)}, u32[]{:S(2)}) collective-permute-start(bf16[2,4,128,128]{3,2,1,0:T(8,128)(2,1)S(1)} %slice.33.rest_0_), channel_id=1, source_target_pairs={{0,16},{4,20},{8,24},{12,28},{16,0},{20,4},{24,8},{28,12},{1,17},{... | collective-permute-start | bytes 786440 | tf_op jit(solution)/shard_map/ppermute | solution.py:322
  12.0 11.7 %collective-permute-start = (bf16[2,4,128,128]{3,2,1,0:T(8,128)(2,1)S(1)}, bf16[2,4,128,128]{3,2,1,0:T(8,128)(2,1)S(1)}, u32[]{:S(2)}, u32[]{:S(2)}) collective-permute-start(bf16[2,4,128,128]{3,2,1,0:T(8,128)(2,1)S(1)} %slice.33.rest_0_), channel_id=1, source_target_pairs={{0,8},{4,12},{8,0},{12,4},{16,24},{20,28},{24,16},{28,20},{1,9},{5... | collective-permute-start | bytes 786440 | tf_op jit(solution)/shard_map/ppermute | solution.py:322
  23.7 102.7 %all-gather.7.cloned.1.call-start = ((), (), s32[]{:S(2)}) async-start(), calls=%async_computation.1 | async-start | bytes 11796480 | tf_op jit(solution)/shard_map/all_gather | solution.py:384
  29.9 1.5 collective-permute-start.3
  29.9 1.9 collective-permute-start.4
  30.4 1.8 collective-permute-start.5
  30.4 2.1 collective-permute-start.6
  44.6 40.3 %collective-permute-start.22 = (s32[520,128]{1,0:T(8,128)}, s32[520,128]{1,0:T(8,128)S(1)}, u32[]{:S(2)}, u32[]{:S(2)}) collective-permute-start(s32[520,128]{1,0:T(8,128)} %get-tuple-element.53), channel_id=1, source_target_pairs={{0,3},{1,2},{2,1},{3,0},{4,7},{5,6},{6,5},{7,4},{8,11},{9,10},{10,... | collective-permute-start | bytes 798728 | tf_op jit(solution)/shard_map/ppermute | solution.py:322
  48.2 37.5 %collective-permute-start.23 = (s32[520,128]{1,0:T(8,128)}, s32[520,128]{1,0:T(8,128)S(1)}, u32[]{:S(2)}, u32[]{:S(2)}) collective-permute-start(s32[520,128]{1,0:T(8,128)} %get-tuple-element.54), channel_id=1, source_target_pairs={{0,2},{1,3},{2,0},{3,1},{4,6},{5,7},{6,4},{7,5},{8,10},{9,11},{10,... | collective-permute-start | bytes 798728 | tf_op jit(solution)/shard_map/ppermute | solution.py:322
  48.2 59.9 %collective-permute-start.24 = (s32[520,128]{1,0:T(8,128)}, s32[520,128]{1,0:T(8,128)S(1)}, u32[]{:S(2)}, u32[]{:S(2)}) collective-permute-start(s32[520,128]{1,0:T(8,128)} %get-tuple-element.55), channel_id=1, source_target_pairs={{0,1},{1,0},{2,3},{3,2},{4,5},{5,4},{6,7},{7,6},{8,9},{9,8},{10,11... | collective-permute-start | bytes 798728 | tf_op jit(solution)/shard_map/ppermute | solution.py:322
  60.1 48.1 %collective-permute-start.7 = (s32[520,128]{1,0:T(8,128)}, s32[520,128]{1,0:T(8,128)S(1)}, u32[]{:S(2)}, u32[]{:S(2)}) collective-permute-start(s32[520,128]{1,0:T(8,128)} %get-tuple-element.57), channel_id=1, source_target_pairs={{0,3},{1,2},{2,1},{3,0},{4,7},{5,6},{6,5},{7,4},{8,11},{9,10},{10,... | collective-permute-start | bytes 798728 | tf_op jit(solution)/shard_map/ppermute | solution.py:322
  63.8 45.1 %collective-permute-start.8 = (s32[520,128]{1,0:T(8,128)}, s32[520,128]{1,0:T(8,128)S(1)}, u32[]{:S(2)}, u32[]{:S(2)}) collective-permute-start(s32[520,128]{1,0:T(8,128)} %get-tuple-element.58), channel_id=1, source_target_pairs={{0,2},{1,3},{2,0},{3,1},{4,6},{5,7},{6,4},{7,5},{8,10},{9,11},{10,... | collective-permute-start | bytes 798728 | tf_op jit(solution)/shard_map/ppermute | solution.py:322
  84.8 27.8 %collective-permute-start.9 = (s32[520,128]{1,0:T(8,128)}, s32[520,128]{1,0:T(8,128)S(1)}, u32[]{:S(2)}, u32[]{:S(2)}) collective-permute-start(s32[520,128]{1,0:T(8,128)} %get-tuple-element.59), channel_id=1, source_target_pairs={{0,1},{1,0},{2,3},{3,2},{4,5},{5,4},{6,7},{7,6},{8,9},{9,8},{10,11... | collective-permute-start | bytes 798728 | tf_op jit(solution)/shard_map/ppermute | solution.py:322
  85.7 64.1 %collective-permute-start.25 = (s32[1032,128]{1,0:T(8,128)}, s32[1032,128]{1,0:T(8,128)S(1)}, u32[]{:S(2)}, u32[]{:S(2)}) collective-permute-start(s32[1032,128]{1,0:T(8,128)} %get-tuple-element.80), channel_id=1, source_target_pairs={{0,3},{1,2},{2,1},{3,0},{4,7},{5,6},{6,5},{7,4},{8,11},{9,10},{10,... | collective-permute-start | bytes 1585160 | tf_op jit(solution)/shard_map/ppermute | solution.py:322
  108.1 69.0 %collective-permute-start.26 = (s32[1032,128]{1,0:T(8,128)}, s32[1032,128]{1,0:T(8,128)S(1)}, u32[]{:S(2)}, u32[]{:S(2)}) collective-permute-start(s32[1032,128]{1,0:T(8,128)} %get-tuple-element.81), channel_id=1, source_target_pairs={{0,2},{1,3},{2,0},{3,1},{4,6},{5,7},{6,4},{7,5},{8,10},{9,11},{10,... | collective-permute-start | bytes 1585160 | tf_op jit(solution)/shard_map/ppermute | solution.py:322
  108.2 68.3 %copy-start.3 = (s32[520,128]{1,0:T(8,128)}, s32[520,128]{1,0:T(8,128)S(1)}, u32[]{:S(2)}) copy-start(s32[520,128]{1,0:T(8,128)S(1)} %collective-permute-done.7.rest_1_.rest_13_) | copy-start | bytes 798724
  108.2 69.0 %collective-permute-start.27 = (s32[1032,128]{1,0:T(8,128)}, s32[1032,128]{1,0:T(8,128)S(1)}, u32[]{:S(2)}, u32[]{:S(2)}) collective-permute-start(s32[1032,128]{1,0:T(8,128)} %get-tuple-element.82), channel_id=1, source_target_pairs={{0,1},{1,0},{2,3},{3,2},{4,5},{5,4},{6,7},{7,6},{8,9},{9,8},{10,11... | collective-permute-start | bytes 1585160 | tf_op jit(solution)/shard_map/ppermute | solution.py:322
  108.9 67.6 %copy-start.4 = (s32[520,128]{1,0:T(8,128)}, s32[520,128]{1,0:T(8,128)S(1)}, u32[]{:S(2)}) copy-start(s32[520,128]{1,0:T(8,128)S(1)} %collective-permute-done.8.rest_2_.rest_14_) | copy-start | bytes 798724
  108.9 71.3 %collective-permute-start.10 = (s32[1032,128]{1,0:T(8,128)}, s32[1032,128]{1,0:T(8,128)S(1)}, u32[]{:S(2)}, u32[]{:S(2)}) collective-permute-start(s32[1032,128]{1,0:T(8,128)} %get-tuple-element.63), channel_id=1, source_target_pairs={{0,3},{1,2},{2,1},{3,0},{4,7},{5,6},{6,5},{7,4},{8,11},{9,10},{10,... | collective-permute-start | bytes 1585160 | tf_op jit(solution)/shard_map/ppermute | solution.py:322
  112.7 63.9 %copy-start.5 = (s32[520,128]{1,0:T(8,128)}, s32[520,128]{1,0:T(8,128)S(1)}, u32[]{:S(2)}) copy-start(s32[520,128]{1,0:T(8,128)S(1)} %collective-permute-done.9.rest_3_.rest_15_) | copy-start | bytes 798724
  112.7 115.4 %collective-permute-start.11 = (s32[1032,128]{1,0:T(8,128)}, s32[1032,128]{1,0:T(8,128)S(1)}, u32[]{:S(2)}, u32[]{:S(2)}) collective-permute-start(s32[1032,128]{1,0:T(8,128)} %get-tuple-element.64), channel_id=1, source_target_pairs={{0,2},{1,3},{2,0},{3,1},{4,6},{5,7},{6,4},{7,5},{8,10},{9,11},{10,... | collective-permute-start | bytes 1585160 | tf_op jit(solution)/shard_map/ppermute | solution.py:322
  149.8 101.8 %copy-start.6 = (s32[1032,128]{1,0:T(8,128)}, s32[1032,128]{1,0:T(8,128)S(1)}, u32[]{:S(2)}) copy-start(s32[1032,128]{1,0:T(8,128)S(1)} %collective-permute-done.25.rest_5_.rest_17_) | copy-start | bytes 1585156
  149.8 101.8 %collective-permute-start.31 = (s32[1288,128]{1,0:T(8,128)}, s32[1288,128]{1,0:T(8,128)S(1)}, u32[]{:S(2)}, u32[]{:S(2)}) collective-permute-start(s32[1288,128]{1,0:T(8,128)} %get-tuple-element.88), channel_id=1, source_target_pairs={{0,3},{1,2},{2,1},{3,0},{4,7},{5,6},{6,5},{7,4},{8,11},{9,10},{10,... | collective-permute-start | bytes 1978376 | tf_op jit(solution)/shard_map/ppermute | solution.py:322
  177.2 93.9 %copy-start.7 = (s32[1032,128]{1,0:T(8,128)}, s32[1032,128]{1,0:T(8,128)S(1)}, u32[]{:S(2)}) copy-start(s32[1032,128]{1,0:T(8,128)S(1)} %collective-permute-done.26.rest_6_.rest_18_) | copy-start | bytes 1585156
  177.2 108.1 %collective-permute-start.32 = (s32[1288,128]{1,0:T(8,128)S(1)}, s32[1288,128]{1,0:T(8,128)S(1)}, u32[]{:S(2)}, u32[]{:S(2)}) collective-permute-start(s32[1288,128]{1,0:T(8,128)S(1)} %copy-done.37), channel_id=1, source_target_pairs={{0,2},{1,3},{2,0},{3,1},{4,6},{5,7},{6,4},{7,5},{8,10},{9,11},{10,... | collective-permute-start | bytes 1978376 | tf_op jit(solution)/shard_map/ppermute | solution.py:322
  177.2 93.9 %copy-start.8 = (s32[1032,128]{1,0:T(8,128)}, s32[1032,128]{1,0:T(8,128)S(1)}, u32[]{:S(2)}) copy-start(s32[1032,128]{1,0:T(8,128)S(1)} %collective-permute-done.27.rest_7_.rest_19_) | copy-start | bytes 1585156
  177.2 108.2 %collective-permute-start.33 = (s32[1288,128]{1,0:T(8,128)S(1)}, s32[1288,128]{1,0:T(8,128)S(1)}, u32[]{:S(2)}, u32[]{:S(2)}) collective-permute-start(s32[1288,128]{1,0:T(8,128)S(1)} %copy-done.36), channel_id=1, source_target_pairs={{0,1},{1,0},{2,3},{3,2},{4,5},{5,4},{6,7},{7,6},{8,9},{9,8},{10,11... | collective-permute-start | bytes 1978376 | tf_op jit(solution)/shard_map/ppermute | solution.py:322
  180.3 90.8 %copy-start = (s32[1032,128]{1,0:T(8,128)}, s32[1032,128]{1,0:T(8,128)S(1)}, u32[]{:S(2)}) copy-start(s32[1032,128]{1,0:T(8,128)S(1)} %collective-permute-done.10.rest_5_.rest_17_) | copy-start | bytes 1585156
  180.3 108.4 %collective-permute-start.28 = (s32[1288,128]{1,0:T(8,128)}, s32[1288,128]{1,0:T(8,128)S(1)}, u32[]{:S(2)}, u32[]{:S(2)}) collective-permute-start(s32[1288,128]{1,0:T(8,128)} %get-tuple-element.84), channel_id=1, source_target_pairs={{0,3},{1,2},{2,1},{3,0},{4,7},{5,6},{6,5},{7,4},{8,11},{9,10},{10,... | collective-permute-start | bytes 1978376 | tf_op jit(solution)/shard_map/ppermute | solution.py:322
  228.1 43.0 %copy-start.1 = (s32[1032,128]{1,0:T(8,128)}, s32[1032,128]{1,0:T(8,128)S(1)}, u32[]{:S(2)}) copy-start(s32[1032,128]{1,0:T(8,128)S(1)} %collective-permute-done.11.rest_6_.rest_18_) | copy-start | bytes 1585156
  228.1 96.8 %collective-permute-start.29 = (s32[1288,128]{1,0:T(8,128)}, s32[1288,128]{1,0:T(8,128)S(1)}, u32[]{:S(2)}, u32[]{:S(2)}) collective-permute-start(s32[1288,128]{1,0:T(8,128)} %get-tuple-element.85), channel_id=1, source_target_pairs={{0,2},{1,3},{2,0},{3,1},{4,6},{5,7},{6,4},{7,5},{8,10},{9,11},{10,... | collective-permute-start | bytes 1978376 | tf_op jit(solution)/shard_map/ppermute | solution.py:322
  251.6 84.3 %collective-permute-start.30 = (s32[1288,128]{1,0:T(8,128)}, s32[1288,128]{1,0:T(8,128)S(1)}, u32[]{:S(2)}, u32[]{:S(2)}) collective-permute-start(s32[1288,128]{1,0:T(8,128)} %get-tuple-element.86), channel_id=1, source_target_pairs={{0,1},{1,0},{2,3},{3,2},{4,5},{5,4},{6,7},{7,6},{8,9},{9,8},{10,11... | collective-permute-start | bytes 1978376 | tf_op jit(solution)/shard_map/ppermute | solution.py:322
  285.2 50.7 %copy-start.43 = (s32[648,128]{1,0:T(8,128)S(1)}, s32[648,128]{1,0:T(8,128)}, u32[]{:S(2)}) copy-start(s32[648,128]{1,0:T(8,128)} %get-tuple-element.72) | copy-start | bytes 995332
  285.3 64.9 %collective-permute-start.12 = (s32[1032,128]{1,0:T(8,128)}, s32[1032,128]{1,0:T(8,128)S(1)}, u32[]{:S(2)}, u32[]{:S(2)}) collective-permute-start(s32[1032,128]{1,0:T(8,128)} %get-tuple-element.65), channel_id=1, source_target_pairs={{0,1},{1,0},{2,3},{3,2},{4,5},{5,4},{6,7},{7,6},{8,9},{9,8},{10,11... | collective-permute-start | bytes 1585160 | tf_op jit(solution)/shard_map/ppermute | solution.py:322
  286.2 91.0 %collective-permute-start.19 = (s32[1288,128]{1,0:T(8,128)}, s32[1288,128]{1,0:T(8,128)S(1)}, u32[]{:S(2)}, u32[]{:S(2)}) collective-permute-start(s32[1288,128]{1,0:T(8,128)} %get-tuple-element.76), channel_id=1, source_target_pairs={{0,3},{1,2},{2,1},{3,0},{4,7},{5,6},{6,5},{7,4},{8,11},{9,10},{10,... | collective-permute-start | bytes 1978376 | tf_op jit(solution)/shard_map/ppermute | solution.py:322
  288.7 50.6 %copy-start.12 = (s32[1288,128]{1,0:T(8,128)}, s32[1288,128]{1,0:T(8,128)S(1)}, u32[]{:S(2)}) copy-start(s32[1288,128]{1,0:T(8,128)S(1)} %collective-permute-done.28.rest_9_.rest_21_) | copy-start | bytes 1978372
  288.7 91.1 %collective-permute-start.20 = (s32[1288,128]{1,0:T(8,128)}, s32[1288,128]{1,0:T(8,128)S(1)}, u32[]{:S(2)}, u32[]{:S(2)}) collective-permute-start(s32[1288,128]{1,0:T(8,128)} %get-tuple-element.77), channel_id=1, source_target_pairs={{0,2},{1,3},{2,0},{3,1},{4,6},{5,7},{6,4},{7,5},{8,10},{9,11},{10,... | collective-permute-start | bytes 1978376 | tf_op jit(solution)/shard_map/ppermute | solution.py:322
  324.9 54.9 %collective-permute-start.21 = (s32[1288,128]{1,0:T(8,128)}, s32[1288,128]{1,0:T(8,128)S(1)}, u32[]{:S(2)}, u32[]{:S(2)}) collective-permute-start(s32[1288,128]{1,0:T(8,128)} %get-tuple-element.78), channel_id=1, source_target_pairs={{0,1},{1,0},{2,3},{3,2},{4,5},{5,4},{6,7},{7,6},{8,9},{9,8},{10,11... | collective-permute-start | bytes 1978376 | tf_op jit(solution)/shard_map/ppermute | solution.py:322
  335.9 15.7 %collective-permute-start.16 = (s32[648,128]{1,0:T(8,128)S(1)}, s32[648,128]{1,0:T(8,128)S(1)}, u32[]{:S(2)}, u32[]{:S(2)}) collective-permute-start(s32[648,128]{1,0:T(8,128)S(1)} %copy-done.43), channel_id=1, source_target_pairs={{0,3},{1,2},{2,1},{3,0},{4,7},{5,6},{6,5},{7,4},{8,11},{9,10},{10,... | collective-permute-start | bytes 995336 | tf_op jit(solution)/shard_map/ppermute | solution.py:322
  350.2 42.6 %collective-permute-start.17 = (s32[648,128]{1,0:T(8,128)S(1)}, s32[648,128]{1,0:T(8,128)S(1)}, u32[]{:S(2)}, u32[]{:S(2)}) collective-permute-start(s32[648,128]{1,0:T(8,128)S(1)} %copy-done.42), channel_id=1, source_target_pairs={{0,2},{1,3},{2,0},{3,1},{4,6},{5,7},{6,4},{7,5},{8,10},{9,11},{10,... | collective-permute-start | bytes 995336 | tf_op jit(solution)/shard_map/ppermute | solution.py:322
  351.6 45.7 %copy-start.22 = (s32[648,128]{1,0:T(8,128)}, s32[648,128]{1,0:T(8,128)S(1)}, u32[]{:S(2)}) copy-start(s32[648,128]{1,0:T(8,128)S(1)} %collective-permute-done.16.rest_9_.rest_21_) | copy-start | bytes 995332
  351.6 45.7 %collective-permute-start.18 = (s32[648,128]{1,0:T(8,128)S(1)}, s32[648,128]{1,0:T(8,128)S(1)}, u32[]{:S(2)}, u32[]{:S(2)}) collective-permute-start(s32[648,128]{1,0:T(8,128)S(1)} %copy-done.41), channel_id=1, source_target_pairs={{0,1},{1,0},{2,3},{3,2},{4,5},{5,4},{6,7},{7,6},{8,9},{9,8},{10,11... | collective-permute-start | bytes 995336 | tf_op jit(solution)/shard_map/ppermute | solution.py:322
  377.3 27.8 %collective-permute-start.13 = (s32[648,128]{1,0:T(8,128)S(1)}, s32[648,128]{1,0:T(8,128)S(1)}, u32[]{:S(2)}, u32[]{:S(2)}) collective-permute-start(s32[648,128]{1,0:T(8,128)S(1)} %copy-done.40), channel_id=1, source_target_pairs={{0,3},{1,2},{2,1},{3,0},{4,7},{5,6},{6,5},{7,4},{8,11},{9,10},{10,... | collective-permute-start | bytes 995336 | tf_op jit(solution)/shard_map/ppermute | solution.py:322
  379.8 31.7 %collective-permute-start.14 = (s32[648,128]{1,0:T(8,128)S(1)}, s32[648,128]{1,0:T(8,128)S(1)}, u32[]{:S(2)}, u32[]{:S(2)}) collective-permute-start(s32[648,128]{1,0:T(8,128)S(1)} %copy-done.39), channel_id=1, source_target_pairs={{0,2},{1,3},{2,0},{3,1},{4,6},{5,7},{6,4},{7,5},{8,10},{9,11},{10,... | collective-permute-start | bytes 995336 | tf_op jit(solution)/shard_map/ppermute | solution.py:322
  379.9 31.6 %collective-permute-start.15 = (s32[648,128]{1,0:T(8,128)S(1)}, s32[648,128]{1,0:T(8,128)S(1)}, u32[]{:S(2)}, u32[]{:S(2)}) collective-permute-start(s32[648,128]{1,0:T(8,128)S(1)} %copy-done.38), channel_id=1, source_target_pairs={{0,1},{1,0},{2,3},{3,2},{4,5},{5,4},{6,7},{7,6},{8,9},{9,8},{10,11... | collective-permute-start | bytes 995336 | tf_op jit(solution)/shard_map/ppermute | solution.py:322
  (32 other events, 454.9 us)
Sparse Core Ops, SparseCore 0:
  23.9 37.1 all-gather.4
  63.0 63.3 all-gather.6
